TPU v7x, 128 devices: a whole 4x4x4 slice. The times are simulated.
128 devices in a mesh: wave: 16 (over z, x_hi, core), lev: 8 (over y, x_lo).
Axes of the slice: x: 4 (x_hi: 2, x_lo: 2; x = x_hi * 2 + x_lo), y: 4, z: 4, core: 2. Of those that a mesh axis runs over, the one named last changes fastest.
Arguments:
- spectra: float32 [320, 136, 2, 384], P('wave', 'lev'), may hold values from -6 to 6
- band_filter: float32 [4, 384], replicated, may hold values from 0.5 to 2
- band_blocks: int32 [4, 12], replicated, may hold values 0 or 1
- legendre: float32 [320, 384, 640], P('wave'), may hold values from -0.3125 to 0.3125
- vert_cov: float32 [4, 32, 136, 136], P(None, 'wave'), may hold values from -0.5 to 0.5
- lat_cov: int32 [640], replicated, may hold values from 0 to 31
Outputs:
- result: float32 [320, 136, 2, 384], P('wave', 'lev')
All inputs are finite; a program needn't handle non-finite values.
Results may differ from a plain program's by a relative error of at most 0.000071.
Values sent between devices are 32-bit elements; how exact they have to be, the bound alone decides.
A program may use at most 256 MiB of HBM per device.

v0:
```python
import jax
import jax.numpy as jnp
from jax import lax
from jax.sharding import PartitionSpec as P


def covary(gridded, cov_all, lat_cov, band_count, lev_count, wave_count):
    total_lat = gridded.shape[0]
    wave_size = lax.axis_size("wave")
    lev_size = lax.axis_size("lev")
    lat_count = total_lat // (wave_size * lev_size)
    packed = gridded.reshape(wave_size, lev_size, -1)
    exchanged = lax.all_to_all(
        lax.all_to_all(packed, "wave", split_axis=0, concat_axis=0, tiled=True),
        "lev",
        split_axis=1,
        concat_axis=1,
        tiled=True,
    )
    exchanged = exchanged.reshape(
        wave_size, lev_size, lat_count, band_count, lev_count, 2, wave_count
    )
    columns = jnp.transpose(exchanged, (3, 2, 1, 4, 5, 0, 6))
    columns = columns.reshape(
        band_count, lat_count, lev_size * lev_count, 2 * wave_size * wave_count
    )
    lat_start = (lax.axis_index("wave") * lev_size + lax.axis_index("lev")) * lat_count
    chosen = lax.dynamic_slice_in_dim(lat_cov, lat_start, lat_count)
    selected = jnp.take(cov_all, chosen, axis=1)
    covaried = jnp.einsum("bpkl,bplx->bpkx", selected, columns, precision=lax.Precision.HIGHEST)
    back = covaried.reshape(band_count, lat_count, lev_size, lev_count, 2, wave_size, wave_count)
    back = jnp.transpose(back, (5, 2, 1, 0, 3, 4, 6)).reshape(wave_size, lev_size, -1)
    returned = lax.all_to_all(
        lax.all_to_all(back, "wave", split_axis=0, concat_axis=0, tiled=True),
        "lev",
        split_axis=1,
        concat_axis=1,
        tiled=True,
    )
    return returned.reshape(total_lat, band_count * lev_count * 2, wave_count)


def apply_bands(spectra, legendre, weights, cov_all, lat_cov):
    wave_count = spectra.shape[0]
    lev_count = spectra.shape[1]
    total_n = spectra.shape[3]
    band_count = weights.shape[1]
    filtered = (spectra[:, None] * weights).reshape(wave_count, -1, total_n)
    gridded = jnp.einsum("mkn,mnp->pkm", filtered, legendre, precision=lax.Precision.HIGHEST)
    returned = covary(gridded, cov_all, lat_cov, band_count, lev_count, wave_count)
    adjoint_out = jnp.einsum("pkm,mnp->mkn", returned, legendre, precision=lax.Precision.HIGHEST)
    adjoint_out = adjoint_out.reshape(wave_count, band_count, lev_count, 2, total_n)
    return jnp.sum(adjoint_out * weights, axis=1)


def local(spectra, band_filter, band_blocks, legendre, vert_cov, lat_cov):
    wave_count = spectra.shape[0]
    total_n = spectra.shape[3]
    block_width = total_n // band_blocks.shape[1]
    first_wave = lax.axis_index("wave") * wave_count
    zonal = first_wave + jnp.arange(wave_count, dtype=jnp.int32)
    waves = jnp.arange(total_n, dtype=jnp.int32)
    triangle = (waves[None, :] >= zonal[:, None]).astype(jnp.float32)
    filters = band_filter * jnp.repeat(band_blocks.astype(jnp.float32), block_width, axis=1)
    weights = (filters[None, :, :] * triangle[:, None, :])[:, :, None, None, :]
    cov_all = lax.all_gather(vert_cov, "wave", axis=1, tiled=True)
    result = apply_bands(spectra, legendre, weights, cov_all, lat_cov)
    return result


def solution(mesh):
    return jax.shard_map(
        local,
        mesh=mesh,
        in_specs=(
            P("wave", "lev", None, None),
            P(),
            P(),
            P("wave", None, None),
            P(None, "wave", None, None),
            P(),
        ),
        out_specs=P("wave", "lev", None, None),
        check_vma=False,
    )
```

profile of v0, /device:TPU:1, one launch (start us, length us, event | category | flops | bytes accessed | tf_op | source)
XLA Modules:
  0.0 889.1 jit_solution(3141994321106592553)
XLA Ops:
  14.2 6.1 mul.62
  20.3 21.4 %convolution_bitcast_fusion = f32[640,136,20]{0,1,2:T(8,128)} fusion(f32[20,136,384]{2,1,0:T(8,128)} %mul.62, f32[20,384,640]{2,1,0:T(8,128)} %param.9), kind=kOutput, calls=%fused_computation.3 | convolution fusion | flops 8021606400 | bytes 30801920 | tf_op jit(solution)/shard_map/mkn,mnp->pkm/dot_general | solution.py:49
  41.7 23.8 %copy.13 = f32[640,136,20]{2,1,0:T(8,128)} copy(f32[640,136,20]{0,1,2:T(8,128)} %convolution_bitcast_fusion) | data formatting | bytes 13926400 | tf_op jit(solution)/shard_map/mkn,mnp->pkm/transpose | solution.py:49
  65.5 24.8 %reshape.59 = f32[16,8,13600]{2,1,0:T(8,128)} reshape(f32[640,136,20]{2,1,0:T(8,128)} %copy.13) | data formatting | bytes 13926400 | tf_op jit(solution)/shard_map/reshape | solution.py:12
  90.3 101.1 %all_to_all.20 = f32[16,8,13600]{2,1,0:T(8,128)S(1)} all-to-all(f32[16,8,13600]{2,1,0:T(8,128)} %reshape.59), channel_id=1, replica_groups=mesh['wave'=16,'lev'=8] {'wave'}, dimensions={0} | all-to-all | bytes 13926400 | tf_op jit(solution)/shard_map/all_to_all | solution.py:14
  195.5 4.8 all-to-all-start.1
  201.1 78.6 %all-to-all-done.1 = f32[16,8,13600]{2,0,1:T(8,128)} async-done(((f32[16,8,13600]{2,0,1:T(8,128)}), f32[16,8,13600]{2,0,1:T(8,128)}, u32[]{:S(2)}, u32[]{:S(2)}) %all-to-all-start.1) | async-done | bytes 6963232 | tf_op jit(solution)/shard_map/all_to_all | solution.py:13
  279.7 8.2 copy.15
  287.9 65.2 %reshape.60 = f32[16,8,5,4,17,2,20]{6,5,4,3,2,1,0:T(2,128)} reshape(f32[16,8,13600]{2,1,0:T(8,128)} %copy.15) | data formatting | bytes 13926400 | tf_op jit(solution)/shard_map/reshape | solution.py:20
  353.0 41.0 %copy.16 = f32[4,5,8,17,2,16,20]{6,5,4,3,2,1,0:T(8,128)} copy(f32[4,5,8,17,2,16,20]{6,4,3,0,1,2,5:T(2,128)} %bitcast.19) | data formatting | bytes 13926400 | tf_op jit(solution)/shard_map/transpose | solution.py:23
  394.1 38.2 %reshape.61 = f32[4,5,136,640]{3,2,1,0:T(8,128)} reshape(f32[4,5,8,17,2,16,20]{6,5,4,3,2,1,0:T(8,128)} %copy.16) | data formatting | bytes 13926400 | tf_op jit(solution)/shard_map/reshape | solution.py:24
  432.3 6.8 gather_fusion
  439.1 11.2 %fusion = f32[4,5,136,640]{3,2,1,0:T(8,128)} fusion(f32[4,5,136,640]{3,2,1,0:T(8,128)} %reshape.61, f32[5,4,136,136]{3,2,1,0:T(8,128)S(1)} %gather_fusion, pred[5]{0:T(512)(128)(4,1)S(1)} %get-tuple-element.5), kind=kOutput, calls=%fused_computation.4 | convolution fusion | flops 2841355520 | bytes 15406085 | tf_op jit(solution)/shard_map/bpkl,bplx->bpkx/dot_general | solution.py:30
  450.3 54.1 %reshape.62 = f32[4,5,8,17,2,16,20]{6,5,4,3,2,1,0:T(8,128)} reshape(f32[4,5,136,640]{3,2,1,0:T(8,128)} %fusion) | data formatting | bytes 13926400 | tf_op jit(solution)/shard_map/reshape | solution.py:31
  504.4 61.4 %copy.25 = f32[4,5,8,17,2,16,20]{6,4,3,0,1,2,5:T(2,128)} copy(f32[4,5,8,17,2,16,20]{6,5,4,3,2,1,0:T(8,128)} %reshape.62) | data formatting | bytes 13926400 | tf_op jit(solution)/shard_map/reshape | solution.py:31
  565.8 55.7 %reshape.63 = f32[16,8,13600]{2,1,0:T(8,128)} reshape(f32[16,8,5,4,17,2,20]{6,5,4,3,2,1,0:T(2,128)} %bitcast.20) | data formatting | bytes 13926400 | tf_op jit(solution)/shard_map/reshape | solution.py:32
  621.5 87.3 %all_to_all.21 = f32[16,8,13600]{2,1,0:T(8,128)S(1)} all-to-all(f32[16,8,13600]{2,1,0:T(8,128)} %reshape.63), channel_id=1, replica_groups=mesh['wave'=16,'lev'=8] {'wave'}, dimensions={0} | all-to-all | bytes 13926400 | tf_op jit(solution)/shard_map/all_to_all | solution.py:34
  710.1 82.8 %all_to_all.22 = f32[16,8,13600]{2,0,1:T(8,128)S(1)} all-to-all(f32[16,8,13600]{2,0,1:T(8,128)S(1)} %copy.19), channel_id=1, replica_groups=mesh['wave'=16,'lev'=8] {'lev'}, dimensions={1} | all-to-all | bytes 13926400 | tf_op jit(solution)/shard_map/all_to_all | solution.py:33
  792.9 5.1 copy.20
  798.0 22.9 %reshape.64 = f32[640,136,20]{2,1,0:T(8,128)} reshape(f32[16,8,13600]{2,1,0:T(8,128)} %copy.20) | data formatting | bytes 13926400 | tf_op jit(solution)/shard_map/reshape | solution.py:40
  820.9 25.7 %copy.21 = f32[640,136,20]{0,1,2:T(8,128)} copy(f32[640,136,20]{2,1,0:T(8,128)} %reshape.64) | data formatting | bytes 13926400 | tf_op jit(solution)/shard_map/reshape | solution.py:40
  846.6 23.1 %fusion.3 = f32[20,136,384]{2,1,0:T(8,128)} fusion(f32[640,136,20]{0,1,2:T(8,128)} %copy.21, f32[20,384,640]{2,1,0:T(8,128)} %param.9), kind=kOutput, calls=%fused_computation.15 | convolution fusion | flops 8021606400 | bytes 30801920 | tf_op jit(solution)/shard_map/pkm,mnp->mkn/dot_general | solution.py:51
  869.7 6.1 reshape.65
  875.8 6.0 multiply_reduce_fusion
  (19 shorter events, 14.0 us)
Async XLA Ops:
  6.5 425.8 %all-gather.2.cloned.1.call-start = ((), (), s32[]{:S(2)}) async-start(), calls=%async_computation.4 | async-start | bytes 18939904 | tf_op jit(solution)/shard_map/all_gather | solution.py:66
  8.9 0.7 copy-start
  195.5 84.2 %all-to-all-start.1 = ((f32[16,8,13600]{2,0,1:T(8,128)}), f32[16,8,13600]{2,0,1:T(8,128)}, u32[]{:S(2)}, u32[]{:S(2)}) async-start(f32[16,8,13600]{2,0,1:T(8,128)} %copy.14), calls=%async_computation.1 | async-start | bytes 14024704 | tf_op jit(solution)/shard_map/all_to_all | solution.py:13
  869.7 6.1 copy-start.1
Sparse Core Ops, SparseCore 0:
  9.8 180.6 all-gather.1
where the time goes:
time: 902 us; the launch traced here: 889 us
  local copies, waits for them, and re-layouts  451 us (50%)
  blocking collectives  271 us (30%)
  waiting for transfers between devices  79.3 us (9%)
  matrix products  55.7 us (6%)
  between operations  13.9 us (2%)
  other arithmetic  12.9 us (1%)
    reshape x2, local copies, waits for them, and re-layouts, covary(): covaried.reshape(band_count, lat_count, lev_size, lev_count, 2, wave_size...  115 us
    all_to_all x1, blocking collectives, covary(): lax.all_to_all(packed, 'wave', split_axis=0, concat_axis=0, tiled=True)  101 us
    all_to_all x1, blocking collectives, covary(): lax.all_to_all(back, 'wave', split_axis=0, concat_axis=0, tiled=True)  87.3 us
    all_to_all x1, blocking collectives, covary(): lax.all_to_all(lax.all_to_all(back, 'wave', split_axis=0, concat_axis=0,...  82.8 us
    all_to_all x1, waiting for transfers between devices, covary(): lax.all_to_all(lax.all_to_all(packed, 'wave', split_axis=0, concat_axis=0...  78.6 us
    reshape x1, local copies, waits for them, and re-layouts, covary(): exchanged.reshape(wave_size, lev_size, lat_count, band_count, lev_count,...  65.2 us
    reshape x1, local copies, waits for them, and re-layouts, covary(): jnp.transpose(back, (5, 2, 1, 0, 3, 4, 6)).reshape(wave_size, lev_size, -1)  55.7 us
    reshape x2, local copies, waits for them, and re-layouts, covary(): return returned.reshape(total_lat, band_count * lev_count * 2, wave_count)  48.6 us
  transfers between devices with their start and end apart: 2, of which 1 were waited for; matrix products, arithmetic and copies ran while one was open for 27% of the time, Pallas kernels for 0%

commit v1 on v0

v1 whole, which is shorter than its diff:
```python
import functools
import jax, jax.numpy as jnp
from jax import lax
from jax.experimental import pallas as pl
from jax.experimental.pallas import tpu as pltpu

F32, BF = jnp.float32, jnp.bfloat16
HALF_BLOCK = 544
BLOCK = 1248

NT = (((1,), (1,)), ((), ()))

def split(x):
    hi = x.astype(BF)
    lo = (x - hi.astype(F32)).astype(BF)
    return hi, lo

def dot_nt(a, b):
    return lax.dot_general(a, b, NT, preferred_element_type=F32)

def k2(starts, rank, w, wt, s_ref, l_hbm, cov_hbm, out_ref,
       lbuf, cov, perm, a_cat, lp_cat, s_cat, g, cv, wcol, lsem, csem, *, phases=4):
    lev = lax.axis_index("lev")
    o = lax.rem(lev, 2)
    m0 = 5 * (lev // 2) + 2 * o
    first = lax.axis_index("wave") * 20 + m0
    lcopy = pltpu.make_async_copy(l_hbm.at[pl.ds(m0, 3)], lbuf, lsem)
    lcopy.start()
    ccopy = pltpu.make_async_copy(cov_hbm, cov, csem)
    ccopy.start()
    for t in range(5):
        row = lax.broadcasted_iota(jnp.int32, (128, 640), 0) + 128 * t
        perm[128 * t:128 * (t + 1), :] = (rank[...] == row).astype(F32).astype(BF)
    for b in range(4):
        wcol[:, 128 * b:128 * (b + 1)] = jnp.broadcast_to(wt[:, b:b + 1], (384, 128))
    lane = lax.broadcasted_iota(jnp.int32, (384, 128), 1)
    wtail = jnp.zeros((384, 128), F32)
    for b in range(4):
        wtail = jnp.where((lane >= 8 * b) & (lane < 8 * b + 8), wcol[:, 128 * b:128 * (b + 1)], wtail)
    wcol[:, 512:640] = wtail
    lcopy.wait()

    def prep(mi, _):
        hi, lo = split(lbuf[mi])
        p = perm[...]
        ahi = dot_nt(p, hi).astype(BF)
        a_cat[mi, :, 0:384] = ahi
        a_cat[mi, :, 384:768] = ahi
        a_cat[mi, :, 768:1152] = dot_nt(p, lo).astype(BF)
        lhi = dot_nt(hi, p).astype(BF)
        lp_cat[mi, :, 0:640] = lhi
        lp_cat[mi, :, 640:1280] = lhi
        lp_cat[mi, :, 1280:1920] = dot_nt(lo, p).astype(BF)
        return 0

    lax.fori_loop(0, 3, prep, 0)

    for s in range(5):
        mi = (s + o) // 2
        tri = (lax.broadcasted_iota(jnp.int32, (1, 384), 1) >= first + mi).astype(F32)
        rows = [s_ref[j, 17 * s:17 * s + 17, :] for j in range(8)]
        full = jnp.concatenate(rows, axis=0)
        for b in range(4):
            wb = w[b:b + 1, :] * tri
            hi, lo = split(full[0:128] * wb)
            s_cat[128 * b:128 * (b + 1), 0:384] = hi
            s_cat[128 * b:128 * (b + 1), 384:768] = lo
            s_cat[128 * b:128 * (b + 1), 768:1152] = hi
        tails = jnp.concatenate([full[128:136] * (w[b:b + 1, :] * tri) for b in range(4)], axis=0)
        tails = jnp.concatenate([tails, tails, tails, jnp.zeros_like(tails)], axis=0)
        hi, lo = split(tails)
        s_cat[512:640, 0:384] = hi
        s_cat[512:640, 384:768] = lo
        s_cat[512:640, 768:1152] = hi

        def fwd(t, _):
            off = pl.multiple_of(t * 128, 128)
            g[s, 0:640, pl.ds(off, 128)] = dot_nt(a_cat[mi], s_cat[pl.ds(off, 128), :])
            return 0
        lax.fori_loop(0, 5, fwd, 0)
        g[s, 640:672, :] = jnp.zeros((32, 640), F32)
    ccopy.wait()

    def covary(c, _):
        lo_row, hi_row = starts[c], starts[c + 1]
        base = (lo_row // 8) * 8
        lane128 = lax.broadcasted_iota(jnp.int32, (1, 128), 1)
        blk, odd = c // 2, lax.rem(c, 2)
        at = HALF_BLOCK * odd
        u = cov[blk, 1088:1224, :]
        group = lane128 // 32
        u = jnp.where(lax.rem(group, 2) == odd, u, pltpu.roll(u, 32, 1))
        u = jnp.concatenate([u[0:128], u[128:136], u[128:136], u[128:136], u[128:136]], axis=0)
        uhi, ulo = split(u)
        ucat = jnp.where(lane128 < 64, uhi.astype(F32), ulo.astype(F32))
        trow = cov[blk, pl.ds(pl.multiple_of(at + 512, 8), 32), :]

        def window(t, _):
            r0 = pl.multiple_of(base + 32 * t, 8)
            x = jnp.concatenate([g[s, pl.ds(r0, 32), :] for s in range(5)], axis=0)
            xhi, xlo = split(x)
            t_hi, t_lo = xhi[:, 512:640].astype(F32), xlo[:, 512:640].astype(F32)
            tcat = jnp.where((lane128 >= 32) & (lane128 < 64), t_lo, t_hi).astype(BF)
            row = r0 + lax.broadcasted_iota(jnp.int32, (32, 1), 0)
            keep = row >= lo_row
            tail_out = jnp.zeros((160, 32), F32)
            lane32 = lax.broadcasted_iota(jnp.int32, (1, 32), 1)
            for b in range(4):
                ub = jnp.where((lax.rem(lane128, 32) >= 8 * b) & (lax.rem(lane128, 32) < 8 * b + 8), ucat, 0.0).astype(BF)
                chi, clo = split(jnp.concatenate([cov[blk, pl.ds(pl.multiple_of(at + 128 * b, 8), 128), :], trow], axis=0))
                xb = xhi[:, 128 * b:128 * b + 128]
                lhs = jnp.concatenate([xb, xlo[:, 128 * b:128 * b + 128], xb, tcat], axis=1)
                rhs = jnp.concatenate([chi, chi, clo, ub], axis=1)
                res = dot_nt(lhs, rhs)
                for s in range(5):
                    old = cv[s, pl.ds(r0, 32), 128 * b:128 * b + 128]
                    cv[s, pl.ds(r0, 32), 128 * b:128 * b + 128] = jnp.where(keep, res[32 * s:32 * s + 32, 0:128], old)
                tail_out = jnp.where((lane32 >= 8 * b) & (lane32 < 8 * b + 8), res[:, 128:160], tail_out)
            for s in range(5):
                old = cv[s, pl.ds(r0, 32), 512:544]
                cv[s, pl.ds(r0, 32), 512:544] = jnp.where(keep, tail_out[32 * s:32 * s + 32], old)
            return 0

        lax.fori_loop(0, (hi_row - base + 31) // 32, window, 0)
        return 0

    for s in range(5):
        cv[s, :, 512:640] = jnp.zeros((672, 128), F32)
    if phases >= 3:
        lax.fori_loop(0, 32, covary, 0)

    if phases >= 4:
      for s in range(5):
        mi = (s + o) // 2
        acc = None
        for b in range(5):
            hi, lo = split(cv[s, 0:640, 128 * b:128 * b + 128])
            rhs = jnp.concatenate([hi, lo, hi], axis=0)
            part = jnp.dot(lp_cat[mi], rhs, preferred_element_type=F32)
            part = part * wcol[:, 128 * b:128 * b + 128]
            if b < 4:
                acc = part if acc is None else acc + part
            else:
                tail = part
        tail = tail + pltpu.roll(tail, 128 - 16, 1)
        tail = tail + pltpu.roll(tail, 128 - 8, 1)
        n = lax.broadcasted_iota(jnp.int32, (384, 1), 0)
        tri = (n >= first + mi).astype(F32)
        main = (acc * tri).T
        tail = (tail * tri).T
        res = jnp.concatenate([main, tail[0:8]], axis=0)
        for j in range(8):
            out_ref[j, 17 * s:17 * s + 17, :] = res[17 * j:17 * j + 17]


def compute(starts, rank, w, wt, s, legendre, cov, phases=4):
    vm = lambda: pl.BlockSpec(memory_space=pltpu.VMEM)
    return pl.pallas_call(
        functools.partial(k2, phases=phases),
        out_shape=jax.ShapeDtypeStruct((8, 85, 384), F32),
        in_specs=[pl.BlockSpec(memory_space=pltpu.SMEM), vm(), vm(), vm(), vm(),
                  pl.BlockSpec(memory_space=pl.ANY), pl.BlockSpec(memory_space=pl.ANY)],
        out_specs=vm(),
        scratch_shapes=[
            pltpu.VMEM((3, 384, 640), F32),
            pltpu.VMEM((16, BLOCK, 128), F32),
            pltpu.VMEM((640, 640), BF),
            pltpu.VMEM((3, 640, 1152), BF),
            pltpu.VMEM((3, 384, 1920), BF),
            pltpu.VMEM((640, 1152), BF),
            pltpu.VMEM((5, 672, 640), F32),
            pltpu.VMEM((5, 672, 640), F32),
            pltpu.VMEM((384, 640), F32),
            pltpu.SemaphoreType.DMA(()),
            pltpu.SemaphoreType.DMA(()),
        ],
        compiler_params=pltpu.CompilerParams(vmem_limit_bytes=61 * 2**20),
    )(starts, rank, w, wt, s, legendre, cov)


def pack_cov(vc):
    t = jnp.transpose(vc, (1, 0, 2, 3))
    main = t[:, :, :128, :128].reshape(2, 512, 128)
    rows = t[:, :, 128:, :128].reshape(2, 32, 128)
    u = jnp.transpose(t[:, :, :, 128:], (2, 0, 1, 3)).reshape(136, 64)
    u = jnp.concatenate([u, u], axis=1)
    top = jnp.concatenate([main, rows], axis=1).reshape(2 * HALF_BLOCK, 128)
    return jnp.concatenate([top, u, jnp.zeros((BLOCK - 1224, 128), F32)], axis=0)


def order(lat_cov):
    lat = lat_cov.astype(jnp.int32)
    p = jnp.arange(640, dtype=jnp.int32)
    before = (lat[:, None] < lat[None, :]) | ((lat[:, None] == lat[None, :]) & (p[:, None] < p[None, :]))
    rank = jnp.sum(before.astype(jnp.int32), axis=0)[None, :]
    starts = jnp.sum((lat[:, None] < jnp.arange(40, dtype=jnp.int32)[None, :]).astype(jnp.int32), axis=0)
    return rank, starts
QUARTER = BLOCK // 4
HALF = BLOCK // 2


def place():
    wave, lev = lax.axis_index("wave"), lax.axis_index("lev")
    return wave // 4, lax.rem(wave // 2, 2), lax.rem(wave, 2), lev // 2, lax.rem(lev, 2)


def at(z, xh, core, y, xl):
    return {"wave": (z * 2 + xh) * 2 + core, "lev": y * 2 + xl}


def greet(peers):
    barrier = pltpu.get_barrier_semaphore()
    for peer in peers:
        pl.semaphore_signal(barrier, inc=1, device_id=peer, device_id_type=pl.DeviceIdType.MESH)
    pl.semaphore_wait(barrier, len(peers))


def exchange_starts(src, dst, send, recv):
    me = lax.axis_index("lev")
    copies = []
    for step in (4, 3, 5, 2, 6, 1, 7):
        to = lax.rem(me + step, 8)
        copies.append(pltpu.make_async_remote_copy(
            src_ref=src.at[to], dst_ref=dst.at[me], send_sem=send.at[step - 1], recv_sem=recv.at[step - 1],
            device_id={"lev": to}, device_id_type=pl.DeviceIdType.MESH))
    return copies


def lev_peers():
    me = lax.axis_index("lev")
    return [{"lev": lax.rem(me + step, 8)} for step in range(1, 8)]


def gather_kernel(spec_ref, own_ref, s_out, cov_out, a_send, a_recv, c_send, c_recv, l_sem):
    z, xh, core, y, xl = place()
    me = lax.axis_index("lev")
    zu, zd, z2 = lax.rem(z + 1, 4), lax.rem(z + 3, 4), lax.rem(z + 2, 4)
    yu, yd, y2 = lax.rem(y + 1, 4), lax.rem(y + 3, 4), lax.rem(y + 2, 4)
    up, down = at(zu, xh, core, y, xl), at(zd, xh, core, y, xl)
    cross = at(z, 1 - xh, core, y, 1 - xl)
    yup, ydown = at(z, xh, core, yu, xl), at(z, xh, core, yd, xl)
    twin = at(z, xh, 1 - core, y, xl)
    greet(lev_peers() + [up, down, cross, twin])

    def block(zz, xx, kk=None):
        return (zz * 2 + xx) * 2 + (core if kk is None else kk)

    own = block(z, xh)
    ids = {}
    started = []

    def piece(blk, row, count):
        return cov_out.at[blk, pl.ds(pl.multiple_of(row, 8), count)]

    def send(name, target, blk, row, count, src=None):
        n = ids.setdefault(name, len(ids))
        ref = piece(blk, row, count)
        copy = pltpu.make_async_remote_copy(
            src_ref=ref if src is None else src.at[pl.ds(pl.multiple_of(row, 8), count)], dst_ref=ref,
            send_sem=c_send.at[n], recv_sem=c_recv.at[n], device_id=target, device_id_type=pl.DeviceIdType.MESH)
        copy.start()
        started.append(copy)

    def arrived(name, blk, row, count):
        n = ids[name]
        ref = piece(blk, row, count)
        pltpu.make_async_remote_copy(
            src_ref=ref, dst_ref=ref, send_sem=c_send.at[n], recv_sem=c_recv.at[n],
            device_id=twin, device_id_type=pl.DeviceIdType.MESH).wait_recv()

    swaps = exchange_starts(spec_ref, s_out, a_send, a_recv)
    for copy in swaps:
        copy.start()
    locals_ = [pltpu.make_async_copy(spec_ref.at[me], s_out.at[me], l_sem.at[0]),
               pltpu.make_async_copy(own_ref, cov_out.at[own], l_sem.at[1])]
    for copy in locals_:
        copy.start()
    send("x0", cross, own, QUARTER * y, QUARTER, own_ref)
    send("u0", up, own, 0, HALF, own_ref)
    send("d1", down, own, HALF, HALF, own_ref)
    send("u1", up, own, HALF, HALF, own_ref)
    send("d0", down, own, 0, HALF, own_ref)
    send("t0", twin, own, 0, BLOCK, own_ref)

    columns = (z, zd, zu, z2)

    def spread(n):
        blk = block(columns[n], 1 - xh)
        arrived(f"x{n}", blk, QUARTER * y, QUARTER)
        send(f"yu{n}", yup, blk, QUARTER * y, QUARTER)
        send(f"yd{n}", ydown, blk, QUARTER * y, QUARTER)

    def relay(n):
        blk = block(columns[n], 1 - xh)
        arrived(f"yu{n}", blk, QUARTER * yd, QUARTER)
        if n % 2 == 0:
            send(f"yf{n}", yup, blk, QUARTER * yd, QUARTER)
        arrived(f"yd{n}", blk, QUARTER * yu, QUARTER)
        if n % 2 == 1:
            send(f"yf{n}", ydown, blk, QUARTER * yu, QUARTER)

    def finish(n):
        blk = block(columns[n], 1 - xh)
        arrived(f"yf{n}", blk, QUARTER * y2, QUARTER)
        send(f"v{n}", twin, blk, 0, BLOCK)

    spread(0)
    arrived("u0", block(zd, xh), 0, HALF)
    send("uf", up, block(zd, xh), 0, HALF)
    arrived("d1", block(zu, xh), HALF, HALF)
    send("df", down, block(zu, xh), HALF, HALF)
    relay(0)
    arrived("u1", block(zd, xh), HALF, HALF)
    send("x1", cross, block(zd, xh), QUARTER * y, QUARTER)
    send("t1", twin, block(zd, xh), 0, BLOCK)
    arrived("d0", block(zu, xh), 0, HALF)
    send("x2", cross, block(zu, xh), QUARTER * y, QUARTER)
    send("t2", twin, block(zu, xh), 0, BLOCK)
    spread(1)
    spread(2)
    arrived("uf", block(z2, xh), 0, HALF)
    arrived("df", block(z2, xh), HALF, HALF)
    send("x3", cross, block(z2, xh), QUARTER * y, QUARTER)
    send("t3", twin, block(z2, xh), 0, BLOCK)
    finish(0)
    relay(1)
    relay(2)
    spread(3)
    finish(1)
    finish(2)
    relay(3)
    finish(3)
    for copy in locals_:
        copy.wait()
    for copy in swaps:
        copy.wait()
    for n in range(4):
        arrived(f"t{n}", block(columns[n], xh, 1 - core), 0, BLOCK)
        arrived(f"v{n}", block(columns[n], 1 - xh, 1 - core), 0, BLOCK)
    for copy in started:
        copy.wait_send()


def gather(spec, own):
    hbm = pl.BlockSpec(memory_space=pl.ANY)
    return pl.pallas_call(
        gather_kernel,
        out_shape=(jax.ShapeDtypeStruct(spec.shape, F32), jax.ShapeDtypeStruct((16, BLOCK, 128), F32)),
        in_specs=[hbm, hbm],
        out_specs=(hbm, hbm),
        scratch_shapes=[pltpu.SemaphoreType.DMA((7,)), pltpu.SemaphoreType.DMA((7,)),
                        pltpu.SemaphoreType.DMA((30,)), pltpu.SemaphoreType.DMA((30,)),
                        pltpu.SemaphoreType.DMA((2,))],
        compiler_params=pltpu.CompilerParams(collective_id=0, has_side_effects=True),
    )(spec, own)


def return_kernel(src, dst, a_send, a_recv, l_sem):
    me = lax.axis_index("lev")
    greet(lev_peers())
    swaps = exchange_starts(src, dst, a_send, a_recv)
    for copy in swaps:
        copy.start()
    own = pltpu.make_async_copy(src.at[me], dst.at[me], l_sem)
    own.start()
    own.wait()
    for copy in swaps:
        copy.wait()


def give_back(x):
    hbm = pl.BlockSpec(memory_space=pl.ANY)
    return pl.pallas_call(
        return_kernel,
        out_shape=jax.ShapeDtypeStruct(x.shape, F32),
        in_specs=[hbm],
        out_specs=hbm,
        scratch_shapes=[pltpu.SemaphoreType.DMA((7,)), pltpu.SemaphoreType.DMA((7,)), pltpu.SemaphoreType.DMA(())],
        compiler_params=pltpu.CompilerParams(collective_id=1, has_side_effects=True),
    )(x)


def local(spectra, band_filter, band_blocks, legendre, vert_cov, lat_cov):
    rank, starts = order(lat_cov)
    w = band_filter * jnp.repeat(band_blocks.astype(F32), 32, axis=1)
    wt = w.T
    packed = pack_cov(vert_cov)
    spec = jnp.transpose(spectra, (0, 2, 1, 3)).reshape(8, 85, 384)
    s, cov = gather(spec, packed)
    out = compute(starts, rank, w, wt, s, legendre, cov)
    back = give_back(out).reshape(20, 2, 17, 384)
    return jnp.transpose(back, (0, 2, 1, 3))


def solution(mesh):
    P = jax.sharding.PartitionSpec
    return jax.shard_map(
        local,
        mesh=mesh,
        in_specs=(P("wave", "lev", None, None), P(), P(), P("wave", None, None), P(None, "wave", None, None), P()),
        out_specs=P("wave", "lev", None, None),
        check_vma=False,
    )
```

time: 902 us -> 135 us (0.15); the launches traced: 889 us -> 135 us
  local copies, waits for them, and re-layouts: 451 us -> 7.57 us
  blocking collectives: 271 us -> 0 us
  Pallas kernels: 0 us -> 125 us
  waiting for transfers between devices: 79.3 us -> 0 us
  matrix products: 55.7 us -> 0 us
  between operations: 13.9 us -> 0.16 us
  other arithmetic: 12.9 us -> 2.11 us
    reshape x10 -> x4, local copies, waits for them, and re-layouts: 354 us -> 2.63 us  [the longest x1 1.38 us: local(): back = give_back(out).reshape(20, 2, 17, 384)]
    all_to_all x3 -> x0, blocking collectives: 271 us -> none  [the longest x1 101 us: covary(): lax.all_to_all(packed, 'wave', split_axis=0, concat_axis=0, tiled=True)]
    pallas_call x0 -> x3, Pallas kernels: none -> 125 us  [the longest x1 54.9 us: gather(): pl.pallas_call(gather_kernel, out_shape=(jax.ShapeDtypeStruct(spec.shape,...]
    all_to_all x1 -> x0, waiting for transfers between devices: 78.6 us -> none  [covary(): lax.all_to_all(lax.all_to_all(packed, 'wave', split_axis=0, concat_axis=0...]
    transpose x2 -> x4, local copies, waits for them, and re-layouts: 64.8 us -> 1.95 us  [the longest x1 1.5 us: local(): return jnp.transpose(back, (0, 2, 1, 3))]
    dot_general x3 -> x0, matrix products: 55.7 us -> none  [the longest x1 23.1 us: apply_bands(): jnp.einsum('pkm,mnp->mkn', returned, legendre, precision=lax.Precision.HI...]
    all_to_all x4 -> x0, local copies, waits for them, and re-layouts: 18.8 us -> none  [the longest x1 8.16 us: covary(): lax.all_to_all(lax.all_to_all(packed, 'wave', split_axis=0, concat_axis=0...]
  transfers between devices with their start and end apart: 2 -> 0, of which waited for: 1 -> 0; matrix products, arithmetic and copies ran while one was open for 27% -> 0% of each run, Pallas kernels for 0% -> 0%
where the time goes in v1:
time: 135 us
  Pallas kernels  125 us (93%)
  local copies, waits for them, and re-layouts  7.57 us (6%)
  other arithmetic  2.11 us (2%)
    pallas_call x1, Pallas kernels, gather(): pl.pallas_call(gather_kernel, out_shape=(jax.ShapeDtypeStruct(spec.shape,...  54.9 us
    pallas_call x1, Pallas kernels, compute(): pl.pallas_call(functools.partial(k2, phases=phases), out_shape=jax.ShapeD...  52.7 us
    pallas_call x1, Pallas kernels, give_back(): pl.pallas_call(return_kernel, out_shape=jax.ShapeDtypeStruct(x.shape, F32...  17.3 us

profile of v1, /device:TPU:1, one launch (start us, length us, event | category | flops | bytes accessed | tf_op | source)
XLA Modules:
  0.0 134.7 jit_solution(1719780244019093706)
XLA Ops:
  0.0 1.3 copy.32
  1.4 0.0 copy-start.1
  1.5 0.3 copy.26
  1.8 0.1 copy.27
  1.9 0.1 pad.3.clone
  2.0 1.1 maximum_maximum_fusion.own_ref
  3.1 0.0 copy-done.1
  3.1 0.1 copy.24
  3.2 1.1 reshape.24.spec_ref
  4.3 54.9 %shard_map.64 = (f32[8,85,384]{2,1,0:T(8,128)}, f32[16,1248,128]{2,1,0:T(8,128)}) custom-call(f32[8,85,384]{2,1,0:T(8,128)} %reshape.24.spec_ref, f32[1248,128]{1,0:T(8,128)} %maximum_maximum_fusion.own_ref), custom_call_target="tpu_custom_call" | custom-call | tf_op jit(solution)/shard_map/pallas_call | solution.py:346
  59.2 0.0 copy-done.3
  59.2 0.1 copy.23
  59.4 0.0 copy-done.4
  59.4 0.1 copy.22
  59.5 0.0 copy-start
  59.5 0.7 copy.29.w
  60.2 0.0 copy-done.2
  60.2 0.3 convert_reduce_fusion
  60.6 0.6 broadcast_in_dim.6.rank
  61.2 0.6 convert_reduce_fusion.1.starts
  61.8 52.7 %shard_map.65.src = f32[8,85,384]{2,1,0:T(8,128)} custom-call(s32[40]{0:T(128)} %convert_reduce_fusion.1.starts, s32[1,640]{1,0:T(1,128)} %broadcast_in_dim.6.rank, f32[4,384]{1,0:T(4,128)} %copy.29.w, f32[384,4]{1,0:T(8,128)} %bitcast.21, f32[8,85,384]{2,1,0:T(8,128)} %get-tuple-element.7.s_ref, f32[20,384,640]{2,1,0:T(8,128)} %l_hbm.1, ...), custom_call_target="tpu_custom_call" | custom-call | tf_op jit(solution)/shard_map/pallas_call | solution.py:158
  114.5 17.3 %shard_map.66 = f32[8,85,384]{2,1,0:T(8,128)} custom-call(f32[8,85,384]{2,1,0:T(8,128)} %shard_map.65.src), custom_call_target="tpu_custom_call" | custom-call | tf_op jit(solution)/shard_map/pallas_call | solution.py:373
  131.8 1.4 %reshape.29 = f32[20,2,17,384]{3,2,1,0:T(8,128)S(1)} reshape(f32[8,85,384]{2,1,0:T(8,128)} %shard_map.66) | data formatting | bytes 2088960 | tf_op jit(solution)/shard_map/reshape | solution.py:391
  133.2 1.5 %copy.30 = f32[20,17,2,384]{3,2,1,0:T(2,128)} copy(f32[20,17,2,384]{3,1,2,0:T(8,128)S(1)} %bitcast.15) | data formatting | bytes 2088960 | tf_op jit(solution)/shard_map/transpose | solution.py:392
  (11 shorter events, 0.1 us)
Async XLA Ops:
  1.4 1.6 %copy-start.1 = (f32[20,17,2,384]{3,2,1,0:T(2,128)S(1)}, f32[20,17,2,384]{3,2,1,0:T(2,128)}, u32[]{:S(2)}) copy-start(f32[20,17,2,384]{3,2,1,0:T(2,128)} %param.6) | copy-start | bytes 3133444
  4.3 54.9 %copy-start.3 = (f32[4,384]{1,0:T(4,128)S(1)}, f32[4,384]{1,0:T(4,128)}, u32[]{:S(2)}) copy-start(f32[4,384]{1,0:T(4,128)} %param.7) | copy-start | bytes 18436
  4.3 55.0 %copy-start.4 = (s32[4,12]{1,0:T(4,128)S(1)}, s32[4,12]{1,0:T(4,128)}, u32[]{:S(2)}) copy-start(s32[4,12]{1,0:T(4,128)} %param.8) | copy-start | bytes 580
  4.3 55.9 %copy-start.2 = (s32[640]{0:T(1024)S(1)}, s32[640]{0:T(1024)}, u32[]{:S(2)}) copy-start(s32[640]{0:T(1024)} %param.11) | copy-start | bytes 7684
  59.5 2.3 %copy-start = (f32[4,384]{0,1:T(8,128)}, f32[4,384]{0,1:T(8,128)S(1)}, u32[]{:S(2)}) copy-start(f32[4,384]{0,1:T(8,128)S(1)} %bitcast_multiply_fusion) | copy-start | bytes 18436

commit v2 on v0

v2 whole, which is shorter than its diff:
```python
import functools
import jax
import jax.numpy as jnp
from jax import lax
from jax.experimental import pallas as pl
from jax.experimental.pallas import tpu as pltpu

F32, BF = jnp.float32, jnp.bfloat16
NT = (((1,), (1,)), ((), ()))
MESH = pl.DeviceIdType.MESH

HALF_BLOCK = 544
BLOCK = 1248
DIRECT = 480
REST = BLOCK - DIRECT
QUARTER = REST // 4


def split(x):
    hi = x.astype(BF)
    return hi, (x - hi.astype(F32)).astype(BF)


def dot_nt(a, b):
    return lax.dot_general(a, b, NT, preferred_element_type=F32)


def pack_cov(vc):
    t = jnp.transpose(vc, (1, 0, 2, 3))
    main = t[:, :, :128, :128].reshape(2, 512, 128)
    rows = t[:, :, 128:, :128].reshape(2, 32, 128)
    u = jnp.transpose(t[:, :, :, 128:], (2, 0, 1, 3)).reshape(136, 64)
    u = jnp.concatenate([u, u], axis=1)
    top = jnp.concatenate([main, rows], axis=1).reshape(2 * HALF_BLOCK, 128)
    return jnp.concatenate([top, u, jnp.zeros((BLOCK - 1224, 128), F32)], axis=0)


def place():
    wave, lev = lax.axis_index("wave"), lax.axis_index("lev")
    return wave // 4, lax.rem(wave // 2, 2), lax.rem(wave, 2), lev // 2, lax.rem(lev, 2)


def at(z, xh, core, y, xl):
    return {"wave": (z * 2 + xh) * 2 + core, "lev": y * 2 + xl}


def lev_peers():
    me = lax.axis_index("lev")
    return [{"lev": lax.rem(me + step, 8)} for step in range(1, 8)]


def greet(peers):
    barrier = pltpu.get_barrier_semaphore()
    for peer in peers:
        pl.semaphore_signal(barrier, inc=1, device_id=peer, device_id_type=MESH)


def met(peers):
    pl.semaphore_wait(pltpu.get_barrier_semaphore(), len(peers))


class Exchange:
    def __init__(self, src, dst, relay, send, recv):
        wave, me = lax.axis_index("wave"), lax.axis_index("lev")
        y, xl = me // 2, lax.rem(me, 2)

        def lev(dy, dx):
            return lax.rem(y + dy, 4) * 2 + (lax.rem(xl + dx, 2))

        def copy(n, source, target, to):
            return pltpu.make_async_remote_copy(
                src_ref=source, dst_ref=target, send_sem=send.at[n], recv_sem=recv.at[n],
                device_id={"wave": wave, "lev": to}, device_id_type=MESH)

        far = lev(2, 1)
        self.over = copy(0, src.at[far], relay, lev(3, 0))
        self.plain = [copy(1 + n, src.at[lev(dy, dx)], dst.at[me], lev(dy, dx))
                      for n, (dy, dx) in enumerate(((2, 0), (1, 1), (3, 1), (1, 0), (3, 0), (0, 1)))]
        self.on = copy(7, relay, dst.at[lev(1, 0)], lev(3, 1))

    def start(self):
        self.over.start()
        for c in self.plain:
            c.start()

    def hand_on(self):
        self.over.wait_recv()
        self.on.start()

    def finish(self):
        for c in self.plain:
            c.wait_recv()
        self.on.wait_recv()

    def sent(self):
        self.over.wait_send()
        for c in self.plain:
            c.wait_send()
        self.on.wait_send()


def part():
    lev = lax.axis_index("lev")
    o = lax.rem(lev, 2)
    m0 = 5 * (lev // 2) + 2 * o
    return m0, o, lax.axis_index("wave") * 20 + m0


def first_kernel(spec, own_ref, lat, w, leg, cov_out, g_out, lp_out,
                 s_in, relay, lbuf, perm, a_cat, lp, s_cat, g,
                 a_send, a_recv, c_send, c_recv, l_sem, o_sem):
    z, xh, core, y, xl = place()
    me = lax.axis_index("lev")
    zu, zd, z2 = lax.rem(z + 1, 4), lax.rem(z + 3, 4), lax.rem(z + 2, 4)
    yu, yd, y2 = lax.rem(y + 1, 4), lax.rem(y + 3, 4), lax.rem(y + 2, 4)
    up, down = at(zu, xh, core, y, xl), at(zd, xh, core, y, xl)
    cross = at(z, 1 - xh, core, y, 1 - xl)
    yup, ydown = at(z, xh, core, yu, xl), at(z, xh, core, yd, xl)
    twin = at(z, xh, 1 - core, y, xl)
    peers = lev_peers() + [up, down, cross, twin]
    m0, o, first = part()
    greet(peers)
    lcopy = pltpu.make_async_copy(leg.at[pl.ds(m0, 3)], lbuf, l_sem.at[0])
    lcopy.start()

    row = jnp.broadcast_to(lat[...], (8, 640)).astype(F32)
    column = row.T[:, 0:1]
    mine = row[0:1]
    p_row = lax.broadcasted_iota(jnp.int32, (1, 640), 1)
    rank = jnp.zeros((1, 640), F32)
    for t in range(5):
        c = column[128 * t:128 * t + 128]
        p_col = lax.broadcasted_iota(jnp.int32, (128, 1), 0) + 128 * t
        ahead = (c < mine) | ((c == mine) & (p_col < p_row))
        rank = rank + jnp.sum(ahead.astype(F32), axis=0, keepdims=True)
    for t in range(5):
        place_ = (lax.broadcasted_iota(jnp.int32, (128, 640), 0) + 128 * t).astype(F32)
        perm[128 * t:128 * t + 128, :] = (rank == place_).astype(F32).astype(BF)

    def block(zz, xx, kk=None):
        return (zz * 2 + xx) * 2 + (core if kk is None else kk)

    own = block(z, xh)
    columns = (z, zd, zu, z2)
    O = [block(c, xh) for c in columns]
    X = [block(c, 1 - xh) for c in columns]
    ids, started = {}, []

    def piece(blk, row, count):
        return cov_out.at[blk, pl.ds(pl.multiple_of(row, 8), count)]

    def send(name, target, blk, row, count, src=None):
        n = ids.setdefault(name, len(ids))
        ref = piece(blk, row, count)
        copy = pltpu.make_async_remote_copy(
            src_ref=ref if src is None else src.at[pl.ds(pl.multiple_of(row, 8), count)], dst_ref=ref,
            send_sem=c_send.at[n], recv_sem=c_recv.at[n], device_id=target, device_id_type=MESH)
        copy.start()
        started.append(copy)

    def arrived(name, blk, row, count):
        n = ids[name]
        ref = piece(blk, row, count)
        pltpu.make_async_remote_copy(
            src_ref=ref, dst_ref=ref, send_sem=c_send.at[n], recv_sem=c_recv.at[n],
            device_id=twin, device_id_type=MESH).wait_recv()

    def quarter(n):
        return DIRECT + QUARTER * n

    swap = Exchange(spec, s_in, relay, a_send, a_recv)

    def begin():
        met(peers)
        swap.start()
        send("xs", cross, own, quarter(y), QUARTER, own_ref)
        send("uD", up, own, 0, DIRECT, own_ref)
        send("dD", down, own, 0, DIRECT, own_ref)
        send("t0", twin, own, 0, BLOCK, own_ref)
        for copy in locals_:
            copy.start()

    locals_ = [pltpu.make_async_copy(spec.at[me], s_in.at[me], l_sem.at[1]),
               pltpu.make_async_copy(own_ref, cov_out.at[own], l_sem.at[2])]

    def y_sends(n):
        send(f"yu{n}", yup, X[n], quarter(y), QUARTER)
        send(f"yd{n}", ydown, X[n], quarter(y), QUARTER)

    def step1():
        swap.hand_on()
        send("xD0", cross, own, 0, DIRECT, own_ref)
        arrived("xs", X[0], quarter(y), QUARTER)
        send("us", up, X[0], quarter(y), QUARTER)
        send("ds", down, X[0], quarter(y), QUARTER)
        send("uR", up, own, DIRECT, REST, own_ref)
        send("dR", down, own, DIRECT, REST, own_ref)
        y_sends(0)

    def step2():
        arrived("uD", O[1], 0, DIRECT)
        send("uDf", up, O[1], 0, DIRECT // 2)
        send("xD1", cross, O[1], 0, DIRECT)
        arrived("dD", O[2], 0, DIRECT)
        send("dDf", down, O[2], DIRECT // 2, DIRECT // 2)
        send("xD2", cross, O[2], 0, DIRECT)
        arrived("us", X[1], quarter(y), QUARTER)
        send("usf", up, X[1], quarter(y), QUARTER // 2)
        arrived("ds", X[2], quarter(y), QUARTER)
        send("dsf", down, X[2], quarter(y) + QUARTER // 2, QUARTER // 2)
        y_sends(1)
        y_sends(2)

    def y_relay(n):
        arrived(f"yd{n}", X[n], quarter(yu), QUARTER)
        send(f"yf{n}", ydown, X[n], quarter(yu), QUARTER)

    def step3():
        arrived("uDf", O[3], 0, DIRECT // 2)
        arrived("dDf", O[3], DIRECT // 2, DIRECT // 2)
        send("xD3", cross, O[3], 0, DIRECT)
        arrived("usf", X[3], quarter(y), QUARTER // 2)
        arrived("dsf", X[3], quarter(y) + QUARTER // 2, QUARTER // 2)
        y_sends(3)
        y_relay(0)

    def step4():
        y_relay(1)
        y_relay(2)

    def step5():
        arrived("uR", O[1], DIRECT, REST)
        send("uRf", up, O[1], DIRECT, REST // 2)
        arrived("dR", O[2], DIRECT, REST)
        send("dRf", down, O[2], DIRECT + REST // 2, REST // 2)
        send("t1", twin, O[1], 0, BLOCK)
        send("t2", twin, O[2], 0, BLOCK)
        y_relay(3)

    def whole(n):
        arrived(f"xD{n}", X[n], 0, DIRECT)
        arrived(f"yu{n}", X[n], quarter(yd), QUARTER)
        arrived(f"yf{n}", X[n], quarter(y2), QUARTER)
        send(f"v{n}", twin, X[n], 0, BLOCK)

    def step9():
        arrived("uRf", O[3], DIRECT, REST // 2)
        arrived("dRf", O[3], DIRECT + REST // 2, REST // 2)
        send("t3", twin, O[3], 0, BLOCK)
        whole(3)

    outs = []

    def out(src, dst, n):
        copy = pltpu.make_async_copy(src, dst, o_sem.at[n])
        copy.start()
        outs.append(copy)

    def prep_a(mi):
        hi, lo = split(lbuf[mi])
        p = perm[...]
        ahi = dot_nt(p, hi).astype(BF)
        a_cat[mi, :, 0:384] = ahi
        a_cat[mi, :, 384:768] = ahi
        a_cat[mi, :, 768:1152] = dot_nt(p, lo).astype(BF)

    def prep_b(mi):
        hi, lo = split(lbuf[mi])
        p = perm[...]
        lp[mi, :, 0:640] = dot_nt(hi, p).astype(BF)
        lp[mi, :, 640:1280] = dot_nt(lo, p).astype(BF)
        out(lp.at[mi], lp_out.at[mi], mi)

    def synth(s):
        mi = (s + o) // 2
        tri = (lax.broadcasted_iota(jnp.int32, (1, 384), 1) >= first + mi).astype(F32)
        full = jnp.concatenate([s_in[j, 17 * s:17 * s + 17, :] for j in range(8)], axis=0)
        for b in range(4):
            hi, lo = split(full[0:128] * (w[b:b + 1, :] * tri))
            s_cat[128 * b:128 * (b + 1), 0:384] = hi
            s_cat[128 * b:128 * (b + 1), 384:768] = lo
            s_cat[128 * b:128 * (b + 1), 768:1152] = hi
        tails = jnp.concatenate([full[128:136] * (w[b:b + 1, :] * tri) for b in range(4)], axis=0)
        tails = jnp.concatenate([tails, tails, tails, jnp.zeros_like(tails)], axis=0)
        hi, lo = split(tails)
        s_cat[512:640, 0:384] = hi
        s_cat[512:640, 384:768] = lo
        s_cat[512:640, 768:1152] = hi

        def body(t, _):
            off = pl.multiple_of(t * 128, 128)
            g[s, 0:640, pl.ds(off, 128)] = dot_nt(a_cat[mi], s_cat[pl.ds(off, 128), :])
            return 0

        lax.fori_loop(0, 5, body, 0)
        out(g.at[s], g_out.at[s], 3 + s)

    for s in range(5):
        g[s, 640:672, :] = jnp.zeros((32, 640), F32)
    begin()
    lcopy.wait()
    prep_a(0)
    step1()
    prep_b(0)
    prep_a(1)
    step2()
    prep_b(1)
    prep_a(2)
    step3()
    prep_b(2)
    locals_[0].wait()
    swap.finish()
    synth(0)
    step4()
    synth(1)
    step5()
    synth(2)
    whole(0)
    synth(3)
    whole(1)
    whole(2)
    synth(4)
    step9()
    locals_[1].wait()
    swap.sent()
    for copy in outs:
        copy.wait()
    for n in range(4):
        arrived(f"t{n}", block(columns[n], xh, 1 - core), 0, BLOCK)
        arrived(f"v{n}", block(columns[n], 1 - xh, 1 - core), 0, BLOCK)
    for copy in started:
        copy.wait_send()


def first(spec, own, lat, w, leg):
    hbm = pl.BlockSpec(memory_space=pl.ANY)
    vm = pl.BlockSpec(memory_space=pltpu.VMEM)
    dma = pltpu.SemaphoreType.DMA
    return pl.pallas_call(
        first_kernel,
        out_shape=(jax.ShapeDtypeStruct((16, BLOCK, 128), F32), jax.ShapeDtypeStruct((5, 672, 640), F32),
                   jax.ShapeDtypeStruct((3, 384, 1280), BF)),
        in_specs=[hbm, hbm, vm, vm, hbm],
        out_specs=(hbm, hbm, hbm),
        scratch_shapes=[
            pltpu.VMEM((8, 85, 384), F32),
            pltpu.VMEM((85, 384), F32),
            pltpu.VMEM((3, 384, 640), F32),
            pltpu.VMEM((640, 640), BF),
            pltpu.VMEM((3, 640, 1152), BF),
            pltpu.VMEM((3, 384, 1280), BF),
            pltpu.VMEM((640, 1152), BF),
            pltpu.VMEM((5, 672, 640), F32),
            dma((8,)), dma((8,)), dma((38,)), dma((38,)), dma((3,)), dma((8,)),
        ],
        compiler_params=pltpu.CompilerParams(collective_id=0, has_side_effects=True, vmem_limit_bytes=58 * 2**20),
    )(spec, own, lat, w, leg)


def second_kernel(starts, wt, g_hbm, lp_hbm, cov_hbm, out_ref, cov, lp_cat, g, cv, wcol, gsem, lsem, csem):
    m0, o, first_m = part()
    gcopies = [pltpu.make_async_copy(g_hbm.at[s], g.at[s], gsem.at[s]) for s in range(5)]
    for copy in gcopies:
        copy.start()

    def cov_copy(n):
        return pltpu.make_async_copy(cov_hbm.at[n], cov.at[n], csem.at[n])

    def begin(n, _):
        cov_copy(n).start()
        return 0

    lax.fori_loop(0, 16, begin, 0)
    lcopies = [pltpu.make_async_copy(lp_hbm.at[:, :, pl.ds(src, 640)], lp_cat.at[:, :, pl.ds(dst, 640)], lsem.at[n])
               for n, (src, dst) in enumerate(((0, 0), (0, 640), (640, 1280)))]
    for copy in lcopies:
        copy.start()
    for b in range(4):
        wcol[:, 128 * b:128 * (b + 1)] = jnp.broadcast_to(wt[:, b:b + 1], (384, 128))
    lane = lax.broadcasted_iota(jnp.int32, (384, 128), 1)
    wtail = jnp.zeros((384, 128), F32)
    for b in range(4):
        wtail = jnp.where((lane >= 8 * b) & (lane < 8 * b + 8), wcol[:, 128 * b:128 * (b + 1)], wtail)
    wcol[:, 512:640] = wtail
    for s in range(5):
        cv[s, :, 512:640] = jnp.zeros((672, 128), F32)
    for copy in gcopies:
        copy.wait()

    lane128 = lax.broadcasted_iota(jnp.int32, (1, 128), 1)
    lane32 = lax.broadcasted_iota(jnp.int32, (1, 32), 1)

    def covary(c, _):
        lo_row, hi_row = starts[c], starts[c + 1]
        base = (lo_row // 8) * 8
        blk, odd = c // 2, lax.rem(c, 2)

        @pl.when(odd == 0)
        def _():
            cov_copy(blk).wait()

        top = HALF_BLOCK * odd
        u = cov[blk, 1088:1224, :]
        u = jnp.where(lax.rem(lane128 // 32, 2) == odd, u, pltpu.roll(u, 32, 1))
        u = jnp.concatenate([u[0:128], u[128:136], u[128:136], u[128:136], u[128:136]], axis=0)
        uhi, ulo = split(u)
        ucat = jnp.where(lane128 < 64, uhi.astype(F32), ulo.astype(F32))
        trow = cov[blk, pl.ds(pl.multiple_of(top + 512, 8), 32), :]

        def window(t, _):
            r0 = pl.multiple_of(base + 32 * t, 8)
            x = jnp.concatenate([g[s, pl.ds(r0, 32), :] for s in range(5)], axis=0)
            xhi, xlo = split(x)
            t_hi, t_lo = xhi[:, 512:640].astype(F32), xlo[:, 512:640].astype(F32)
            tcat = jnp.where((lane128 >= 32) & (lane128 < 64), t_lo, t_hi).astype(BF)
            keep = r0 + lax.broadcasted_iota(jnp.int32, (32, 1), 0) >= lo_row
            tail_out = jnp.zeros((160, 32), F32)
            for b in range(4):
                of_b = (lax.rem(lane128, 32) >= 8 * b) & (lax.rem(lane128, 32) < 8 * b + 8)
                ub = jnp.where(of_b, ucat, 0.0).astype(BF)
                main = cov[blk, pl.ds(pl.multiple_of(top + 128 * b, 8), 128), :]
                chi, clo = split(jnp.concatenate([main, trow], axis=0))
                xb = xhi[:, 128 * b:128 * b + 128]
                lhs = jnp.concatenate([xb, xlo[:, 128 * b:128 * b + 128], xb, tcat], axis=1)
                rhs = jnp.concatenate([chi, chi, clo, ub], axis=1)
                res = dot_nt(lhs, rhs)
                for s in range(5):
                    old = cv[s, pl.ds(r0, 32), 128 * b:128 * b + 128]
                    cv[s, pl.ds(r0, 32), 128 * b:128 * b + 128] = jnp.where(keep, res[32 * s:32 * s + 32, 0:128], old)
                tail_out = jnp.where((lane32 >= 8 * b) & (lane32 < 8 * b + 8), res[:, 128:160], tail_out)
            for s in range(5):
                old = cv[s, pl.ds(r0, 32), 512:544]
                cv[s, pl.ds(r0, 32), 512:544] = jnp.where(keep, tail_out[32 * s:32 * s + 32], old)
            return 0

        lax.fori_loop(0, (hi_row - base + 31) // 32, window, 0)
        return 0

    lax.fori_loop(0, 32, covary, 0)
    for copy in lcopies:
        copy.wait()

    for s in range(5):
        mi = (s + o) // 2
        acc = None
        for b in range(5):
            hi, lo = split(cv[s, 0:640, 128 * b:128 * b + 128])
            rhs = jnp.concatenate([hi, lo, hi], axis=0)
            one = jnp.dot(lp_cat[mi], rhs, preferred_element_type=F32)
            one = one * wcol[:, 128 * b:128 * b + 128]
            if b < 4:
                acc = one if acc is None else acc + one
            else:
                tail = one
        tail = tail + pltpu.roll(tail, 128 - 16, 1)
        tail = tail + pltpu.roll(tail, 128 - 8, 1)
        tri = (lax.broadcasted_iota(jnp.int32, (384, 1), 0) >= first_m + mi).astype(F32)
        res = jnp.concatenate([(acc * tri).T, (tail * tri).T[0:8]], axis=0)
        for j in range(8):
            out_ref[j, 17 * s:17 * s + 17, :] = res[17 * j:17 * j + 17]


def second(starts, wt, g, lp, cov):
    hbm = pl.BlockSpec(memory_space=pl.ANY)
    vm = pl.BlockSpec(memory_space=pltpu.VMEM)
    dma = pltpu.SemaphoreType.DMA
    return pl.pallas_call(
        second_kernel,
        out_shape=jax.ShapeDtypeStruct((8, 85, 384), F32),
        in_specs=[pl.BlockSpec(memory_space=pltpu.SMEM), vm, hbm, hbm, hbm],
        out_specs=vm,
        scratch_shapes=[
            pltpu.VMEM((16, BLOCK, 128), F32),
            pltpu.VMEM((3, 384, 1920), BF),
            pltpu.VMEM((5, 672, 640), F32),
            pltpu.VMEM((5, 672, 640), F32),
            pltpu.VMEM((384, 640), F32),
            dma((5,)), dma((3,)), dma((16,)),
        ],
        compiler_params=pltpu.CompilerParams(vmem_limit_bytes=58 * 2**20),
    )(starts, wt, g, lp, cov)


def return_kernel(src, dst, relay, a_send, a_recv, l_sem):
    me = lax.axis_index("lev")
    peers = lev_peers()
    greet(peers)
    met(peers)
    swap = Exchange(src, dst, relay, a_send, a_recv)
    swap.start()
    own = pltpu.make_async_copy(src.at[me], dst.at[me], l_sem)
    own.start()
    swap.hand_on()
    own.wait()
    swap.finish()
    swap.sent()


def give_back(x):
    hbm = pl.BlockSpec(memory_space=pl.ANY)
    dma = pltpu.SemaphoreType.DMA
    return pl.pallas_call(
        return_kernel,
        out_shape=jax.ShapeDtypeStruct(x.shape, F32),
        in_specs=[hbm],
        out_specs=hbm,
        scratch_shapes=[pltpu.VMEM((85, 384), F32), dma((8,)), dma((8,)), dma(())],
        compiler_params=pltpu.CompilerParams(collective_id=1, has_side_effects=True),
    )(x)


def local(spectra, band_filter, band_blocks, legendre, vert_cov, lat_cov):
    w = band_filter * jnp.repeat(band_blocks.astype(F32), 32, axis=1)
    spec = jnp.transpose(spectra, (0, 2, 1, 3)).reshape(8, 85, 384)
    cov, g, lp = first(spec, pack_cov(vert_cov), lat_cov.reshape(1, 640), w, legendre)
    bounds = jnp.arange(40, dtype=jnp.int32)
    starts = jnp.sum((lat_cov[:, None] < bounds[None, :]).astype(jnp.int32), axis=0)
    back = give_back(second(starts, w.T, g, lp, cov)).reshape(20, 2, 17, 384)
    return jnp.transpose(back, (0, 2, 1, 3))


def solution(mesh):
    P = jax.sharding.PartitionSpec
    return jax.shard_map(
        local,
        mesh=mesh,
        in_specs=(P("wave", "lev", None, None), P(), P(), P("wave", None, None), P(None, "wave", None, None), P()),
        out_specs=P("wave", "lev", None, None),
        check_vma=False,
    )
```

time: 902 us -> 113 us (0.13); the launches traced: 889 us -> 112 us
  local copies, waits for them, and re-layouts: 451 us -> 7.59 us
  blocking collectives: 271 us -> 0 us
  Pallas kernels: 0 us -> 102 us
  waiting for transfers between devices: 79.3 us -> 0 us
  matrix products: 55.7 us -> 0 us
  between operations: 13.9 us -> 0.17 us
  other arithmetic: 12.9 us -> 1.77 us
    reshape x10 -> x5, local copies, waits for them, and re-layouts: 354 us -> 3.24 us  [the longest x1 1.38 us: local(): back = give_back(second(starts, w.T, g, lp, cov)).reshape(20, 2, 17, 384)]
    all_to_all x3 -> x0, blocking collectives: 271 us -> none  [the longest x1 101 us: covary(): lax.all_to_all(packed, 'wave', split_axis=0, concat_axis=0, tiled=True)]
    pallas_call x0 -> x3, Pallas kernels: none -> 102 us  [the longest x1 50.2 us: first(): pl.pallas_call(first_kernel, out_shape=(jax.ShapeDtypeStruct((16, BLOCK,...]
    all_to_all x1 -> x0, waiting for transfers between devices: 78.6 us -> none  [covary(): lax.all_to_all(lax.all_to_all(packed, 'wave', split_axis=0, concat_axis=0...]
    transpose x2 -> x4, local copies, waits for them, and re-layouts: 64.8 us -> 1.95 us  [the longest x1 1.5 us: local(): return jnp.transpose(back, (0, 2, 1, 3))]
    dot_general x3 -> x0, matrix products: 55.7 us -> none  [the longest x1 23.1 us: apply_bands(): jnp.einsum('pkm,mnp->mkn', returned, legendre, precision=lax.Precision.HI...]
    all_to_all x4 -> x0, local copies, waits for them, and re-layouts: 18.8 us -> none  [the longest x1 8.16 us: covary(): lax.all_to_all(lax.all_to_all(packed, 'wave', split_axis=0, concat_axis=0...]
  transfers between devices with their start and end apart: 2 -> 0, of which waited for: 1 -> 0; matrix products, arithmetic and copies ran while one was open for 27% -> 0% of each run, Pallas kernels for 0% -> 0%
where the time goes in v2:
time: 113 us; the launch traced here: 112 us
  Pallas kernels  102 us (90%)
  local copies, waits for them, and re-layouts  7.59 us (7%)
  other arithmetic  1.77 us (2%)
    pallas_call x1, Pallas kernels, first(): pl.pallas_call(first_kernel, out_shape=(jax.ShapeDtypeStruct((16, BLOCK,...  50.2 us
    pallas_call x1, Pallas kernels, second(): pl.pallas_call(second_kernel, out_shape=jax.ShapeDtypeStruct((8, 85, 384)...  30.5 us
    pallas_call x1, Pallas kernels, give_back(): pl.pallas_call(return_kernel, out_shape=jax.ShapeDtypeStruct(x.shape, F32...  21.5 us

profile of v2, /device:TPU:1, one launch (start us, length us, event | category | flops | bytes accessed | tf_op | source)
XLA Modules:
  0.0 111.7 jit_solution(16884059546322131031)
XLA Ops:
  0.0 1.3 %copy.32 = f32[4,2,136,136]{3,2,0,1:T(8,128)S(1)} copy(f32[4,2,136,136]{3,2,1,0:T(8,128)} %param.10) | data formatting | bytes 1183744 | tf_op args[4]
  1.5 0.0 copy-start.3
  1.5 0.0 copy-start.4
  1.5 0.3 copy.26
  1.8 0.1 copy.27
  1.9 0.1 pad.3.clone
  2.0 1.1 maximum_maximum_fusion.own_ref
  3.1 0.0 copy-done.3
  3.1 0.1 copy.23
  3.2 0.0 copy-done.4
  3.3 0.1 copy.22
  3.4 0.0 copy-start
  3.4 0.7 copy.29.w
  4.1 0.0 copy-done.1
  4.1 0.1 copy.24
  4.2 0.0 copy-start.2
  4.2 1.2 %reshape.26.spec = f32[8,85,384]{2,1,0:T(8,128)} reshape(f32[20,2,17,384]{3,2,1,0:T(8,128)S(1)} %copy.24) | data formatting | bytes 2088960 | tf_op jit(solution)/shard_map/reshape | solution.py:514
  5.4 0.6 reshape.31.lat
  6.0 50.2 %shard_map.64 = (f32[16,1248,128]{2,1,0:T(8,128)}, f32[5,672,640]{2,1,0:T(8,128)}, bf16[3,384,1280]{2,1,0:T(8,128)(2,1)}) custom-call(f32[8,85,384]{2,1,0:T(8,128)} %reshape.26.spec, f32[1248,128]{1,0:T(8,128)} %maximum_maximum_fusion.own_ref, s32[1,640]{1,0:T(1,128)} %reshape.31.lat, f32[4,384]{1,0:T(4,128)} %copy.29.w, f32[20,384,640]{2,1,0:T(8,128)} %leg.1), custom_call_target="tpu_custom_call" | custom-call | tf_op jit(solution)/shard_map/pallas_call | solution.py:339
  56.2 0.6 convert_reduce_fusion.starts
  56.9 30.5 %shard_map.65.src = f32[8,85,384]{2,1,0:T(8,128)} custom-call(s32[40]{0:T(128)} %convert_reduce_fusion.starts, f32[384,4]{1,0:T(8,128)} %bitcast.21, f32[5,672,640]{2,1,0:T(8,128)} %get-tuple-element.8.g_hbm, bf16[3,384,1280]{2,1,0:T(8,128)(2,1)} %get-tuple-element.9.lp_hbm, f32[16,1248,128]{2,1,0:T(8,128)} %get-tuple-element.10.cov_hbm), custom_call_target="tpu_custom_call" | custom-call | tf_op jit(solution)/shard_map/pallas_call | solution.py:467
  87.3 21.5 %shard_map.66 = f32[8,85,384]{2,1,0:T(8,128)} custom-call(f32[8,85,384]{2,1,0:T(8,128)} %shard_map.65.src), custom_call_target="tpu_custom_call" | custom-call | tf_op jit(solution)/shard_map/pallas_call | solution.py:502
  108.9 1.4 %reshape.32 = f32[20,2,17,384]{3,2,1,0:T(8,128)S(1)} reshape(f32[8,85,384]{2,1,0:T(8,128)} %shard_map.66) | data formatting | bytes 2088960 | tf_op jit(solution)/shard_map/reshape | solution.py:518
  110.2 1.5 %copy.30 = f32[20,17,2,384]{3,2,1,0:T(2,128)} copy(f32[20,17,2,384]{3,1,2,0:T(8,128)S(1)} %bitcast.15) | data formatting | bytes 2088960 | tf_op jit(solution)/shard_map/transpose | solution.py:519
  (10 shorter events, 0.1 us)
Async XLA Ops:
  1.5 1.6 %copy-start.3 = (f32[4,384]{1,0:T(4,128)S(1)}, f32[4,384]{1,0:T(4,128)}, u32[]{:S(2)}) copy-start(f32[4,384]{1,0:T(4,128)} %param.7) | copy-start | bytes 18436
  1.5 1.7 %copy-start.4 = (s32[4,12]{1,0:T(4,128)S(1)}, s32[4,12]{1,0:T(4,128)}, u32[]{:S(2)}) copy-start(s32[4,12]{1,0:T(4,128)} %param.8) | copy-start | bytes 580
  1.8 2.3 %copy-start.1 = (f32[20,17,2,384]{3,2,1,0:T(2,128)S(1)}, f32[20,17,2,384]{3,2,1,0:T(2,128)}, u32[]{:S(2)}) copy-start(f32[20,17,2,384]{3,2,1,0:T(2,128)} %param.6) | copy-start | bytes 3133444
  3.4 0.8 copy-start
  4.2 1.2 %copy-start.2 = (s32[640]{0:T(1024)S(1)}, s32[640]{0:T(1024)}, u32[]{:S(2)}) copy-start(s32[640]{0:T(1024)} %param.11) | copy-start | bytes 7684

commit v3 on v2

--- a/solution.py
+++ b/solution.py
@@ -60,43 +60,27 @@
 
 
 class Exchange:
-    def __init__(self, src, dst, relay, send, recv):
+    def __init__(self, src, dst, send, recv):
         wave, me = lax.axis_index("wave"), lax.axis_index("lev")
         y, xl = me // 2, lax.rem(me, 2)
-
-        def lev(dy, dx):
-            return lax.rem(y + dy, 4) * 2 + (lax.rem(xl + dx, 2))
-
-        def copy(n, source, target, to):
-            return pltpu.make_async_remote_copy(
-                src_ref=source, dst_ref=target, send_sem=send.at[n], recv_sem=recv.at[n],
-                device_id={"wave": wave, "lev": to}, device_id_type=MESH)
-
-        far = lev(2, 1)
-        self.over = copy(0, src.at[far], relay, lev(3, 0))
-        self.plain = [copy(1 + n, src.at[lev(dy, dx)], dst.at[me], lev(dy, dx))
-                      for n, (dy, dx) in enumerate(((2, 0), (1, 1), (3, 1), (1, 0), (3, 0), (0, 1)))]
-        self.on = copy(7, relay, dst.at[lev(1, 0)], lev(3, 1))
+        self.copies = []
+        for n, (dy, dx) in enumerate(((2, 1), (2, 0), (1, 1), (3, 1), (1, 0), (3, 0), (0, 1))):
+            to = lax.rem(y + dy, 4) * 2 + lax.rem(xl + dx, 2)
+            self.copies.append(pltpu.make_async_remote_copy(
+                src_ref=src.at[to], dst_ref=dst.at[me], send_sem=send.at[n], recv_sem=recv.at[n],
+                device_id={"wave": wave, "lev": to}, device_id_type=MESH))
 
     def start(self):
-        self.over.start()
-        for c in self.plain:
+        for c in self.copies:
             c.start()
 
-    def hand_on(self):
-        self.over.wait_recv()
-        self.on.start()
-
     def finish(self):
-        for c in self.plain:
+        for c in self.copies:
             c.wait_recv()
-        self.on.wait_recv()
 
     def sent(self):
-        self.over.wait_send()
-        for c in self.plain:
+        for c in self.copies:
             c.wait_send()
-        self.on.wait_send()
 
 
 def part():
@@ -107,35 +91,21 @@
 
 
 def first_kernel(spec, own_ref, lat, w, leg, cov_out, g_out, lp_out,
-                 s_in, relay, lbuf, perm, a_cat, lp, s_cat, g,
+                 s_in, lbuf, perm, a_cat, lp, s_cat, g,
                  a_send, a_recv, c_send, c_recv, l_sem, o_sem):
     z, xh, core, y, xl = place()
     me = lax.axis_index("lev")
     zu, zd, z2 = lax.rem(z + 1, 4), lax.rem(z + 3, 4), lax.rem(z + 2, 4)
     yu, yd, y2 = lax.rem(y + 1, 4), lax.rem(y + 3, 4), lax.rem(y + 2, 4)
-    up, down = at(zu, xh, core, y, xl), at(zd, xh, core, y, xl)
+    up, down = (at(to, xh, core, y, xl) for to in (zu, zd))
     cross = at(z, 1 - xh, core, y, 1 - xl)
-    yup, ydown = at(z, xh, core, yu, xl), at(z, xh, core, yd, xl)
+    yup, ydown = (at(z, xh, core, to, xl) for to in (yu, yd))
     twin = at(z, xh, 1 - core, y, xl)
     peers = lev_peers() + [up, down, cross, twin]
     m0, o, first = part()
     greet(peers)
     lcopy = pltpu.make_async_copy(leg.at[pl.ds(m0, 3)], lbuf, l_sem.at[0])
     lcopy.start()
-
-    row = jnp.broadcast_to(lat[...], (8, 640)).astype(F32)
-    column = row.T[:, 0:1]
-    mine = row[0:1]
-    p_row = lax.broadcasted_iota(jnp.int32, (1, 640), 1)
-    rank = jnp.zeros((1, 640), F32)
-    for t in range(5):
-        c = column[128 * t:128 * t + 128]
-        p_col = lax.broadcasted_iota(jnp.int32, (128, 1), 0) + 128 * t
-        ahead = (c < mine) | ((c == mine) & (p_col < p_row))
-        rank = rank + jnp.sum(ahead.astype(F32), axis=0, keepdims=True)
-    for t in range(5):
-        place_ = (lax.broadcasted_iota(jnp.int32, (128, 640), 0) + 128 * t).astype(F32)
-        perm[128 * t:128 * t + 128, :] = (rank == place_).astype(F32).astype(BF)
 
     def block(zz, xx, kk=None):
         return (zz * 2 + xx) * 2 + (core if kk is None else kk)
@@ -168,86 +138,95 @@
     def quarter(n):
         return DIRECT + QUARTER * n
 
-    swap = Exchange(spec, s_in, relay, a_send, a_recv)
-
-    def begin():
-        met(peers)
-        swap.start()
-        send("xs", cross, own, quarter(y), QUARTER, own_ref)
-        send("uD", up, own, 0, DIRECT, own_ref)
-        send("dD", down, own, 0, DIRECT, own_ref)
-        send("t0", twin, own, 0, BLOCK, own_ref)
-        for copy in locals_:
-            copy.start()
+    swap = Exchange(spec, s_in, a_send, a_recv)
 
     locals_ = [pltpu.make_async_copy(spec.at[me], s_in.at[me], l_sem.at[1]),
                pltpu.make_async_copy(own_ref, cov_out.at[own], l_sem.at[2])]
+
+    def z_sends(name, blk, row, count, source=None):
+        send(name + "u", up, blk, row, count, source)
+        send(name + "d", down, blk, row, count, source)
+
+    def z_on(name, blocks, row, count):
+        for way, to, blk, first in (("u", up, blocks[1], row), ("d", down, blocks[2], row + count // 2)):
+            send(name + "f" + way, to, blk, first, count // 2)
+
+    def z_got(name, blocks, row, count):
+        arrived(name + "u", blocks[1], row, count)
+        arrived(name + "d", blocks[2], row, count)
+
+    def z_end(name, blocks, row, count):
+        arrived(name + "fu", blocks[3], row, count // 2)
+        arrived(name + "fd", blocks[3], row + count // 2, count // 2)
 
     def y_sends(n):
         send(f"yu{n}", yup, X[n], quarter(y), QUARTER)
         send(f"yd{n}", ydown, X[n], quarter(y), QUARTER)
 
+    def y_on(n):
+        if n % 2 == 0:
+            arrived(f"yu{n}", X[n], quarter(yd), QUARTER)
+            send(f"yf{n}", yup, X[n], quarter(yd), QUARTER)
+        else:
+            arrived(f"yd{n}", X[n], quarter(yu), QUARTER)
+            send(f"yf{n}", ydown, X[n], quarter(yu), QUARTER)
+
+    def begin():
+        met(peers)
+        send("xs", cross, own, quarter(y), QUARTER, own_ref)
+        z_sends("D", own, 0, DIRECT, own_ref)
+        swap.start()
+        send("xD0", cross, own, 0, DIRECT, own_ref)
+        for copy in locals_:
+            copy.start()
+
     def step1():
-        swap.hand_on()
-        send("xD0", cross, own, 0, DIRECT, own_ref)
         arrived("xs", X[0], quarter(y), QUARTER)
-        send("us", up, X[0], quarter(y), QUARTER)
-        send("ds", down, X[0], quarter(y), QUARTER)
-        send("uR", up, own, DIRECT, REST, own_ref)
-        send("dR", down, own, DIRECT, REST, own_ref)
+        z_sends("s", X[0], quarter(y), QUARTER)
         y_sends(0)
 
     def step2():
-        arrived("uD", O[1], 0, DIRECT)
-        send("uDf", up, O[1], 0, DIRECT // 2)
+        z_got("D", O, 0, DIRECT)
+        z_on("D", O, 0, DIRECT)
         send("xD1", cross, O[1], 0, DIRECT)
-        arrived("dD", O[2], 0, DIRECT)
-        send("dDf", down, O[2], DIRECT // 2, DIRECT // 2)
         send("xD2", cross, O[2], 0, DIRECT)
-        arrived("us", X[1], quarter(y), QUARTER)
-        send("usf", up, X[1], quarter(y), QUARTER // 2)
-        arrived("ds", X[2], quarter(y), QUARTER)
-        send("dsf", down, X[2], quarter(y) + QUARTER // 2, QUARTER // 2)
+        z_got("s", X, quarter(y), QUARTER)
+        z_on("s", X, quarter(y), QUARTER)
+        z_sends("R", own, DIRECT, REST, own_ref)
+        send("t0", twin, own, 0, BLOCK, own_ref)
         y_sends(1)
         y_sends(2)
 
-    def y_relay(n):
-        arrived(f"yd{n}", X[n], quarter(yu), QUARTER)
-        send(f"yf{n}", ydown, X[n], quarter(yu), QUARTER)
-
     def step3():
-        arrived("uDf", O[3], 0, DIRECT // 2)
-        arrived("dDf", O[3], DIRECT // 2, DIRECT // 2)
+        z_end("D", O, 0, DIRECT)
         send("xD3", cross, O[3], 0, DIRECT)
-        arrived("usf", X[3], quarter(y), QUARTER // 2)
-        arrived("dsf", X[3], quarter(y) + QUARTER // 2, QUARTER // 2)
+        z_end("s", X, quarter(y), QUARTER)
         y_sends(3)
-        y_relay(0)
+        y_on(0)
 
     def step4():
-        y_relay(1)
-        y_relay(2)
+        y_on(1)
+        y_on(2)
 
     def step5():
-        arrived("uR", O[1], DIRECT, REST)
-        send("uRf", up, O[1], DIRECT, REST // 2)
-        arrived("dR", O[2], DIRECT, REST)
-        send("dRf", down, O[2], DIRECT + REST // 2, REST // 2)
+        z_got("R", O, DIRECT, REST)
+        z_on("R", O, DIRECT, REST)
         send("t1", twin, O[1], 0, BLOCK)
         send("t2", twin, O[2], 0, BLOCK)
-        y_relay(3)
+        y_on(3)
 
     def whole(n):
         arrived(f"xD{n}", X[n], 0, DIRECT)
-        arrived(f"yu{n}", X[n], quarter(yd), QUARTER)
+        if n % 2 == 0:
+            arrived(f"yd{n}", X[n], quarter(yu), QUARTER)
+        else:
+            arrived(f"yu{n}", X[n], quarter(yd), QUARTER)
         arrived(f"yf{n}", X[n], quarter(y2), QUARTER)
         send(f"v{n}", twin, X[n], 0, BLOCK)
 
     def step9():
-        arrived("uRf", O[3], DIRECT, REST // 2)
-        arrived("dRf", O[3], DIRECT + REST // 2, REST // 2)
+        z_end("R", O, DIRECT, REST)
         send("t3", twin, O[3], 0, BLOCK)
-        whole(3)
 
     outs = []
 
@@ -255,6 +234,23 @@
         copy = pltpu.make_async_copy(src, dst, o_sem.at[n])
         copy.start()
         outs.append(copy)
+
+    def order():
+        for s in range(5):
+            g[s, 640:672, :] = jnp.zeros((32, 640), F32)
+        row = jnp.broadcast_to(lat[...], (8, 640)).astype(F32)
+        column = row.T[:, 0:1]
+        mine = row[0:1]
+        p_row = lax.broadcasted_iota(jnp.int32, (1, 640), 1)
+        rank = jnp.zeros((1, 640), F32)
+        for t in range(5):
+            c = column[128 * t:128 * t + 128]
+            p_col = lax.broadcasted_iota(jnp.int32, (128, 1), 0) + 128 * t
+            ahead = (c < mine) | ((c == mine) & (p_col < p_row))
+            rank = rank + jnp.sum(ahead.astype(F32), axis=0, keepdims=True)
+        for t in range(5):
+            place_ = (lax.broadcasted_iota(jnp.int32, (128, 640), 0) + 128 * t).astype(F32)
+            perm[128 * t:128 * t + 128, :] = (rank == place_).astype(F32).astype(BF)
 
     def prep_a(mi):
         hi, lo = split(lbuf[mi])
@@ -295,32 +291,32 @@
         lax.fori_loop(0, 5, body, 0)
         out(g.at[s], g_out.at[s], 3 + s)
 
-    for s in range(5):
-        g[s, 640:672, :] = jnp.zeros((32, 640), F32)
     begin()
+    order()
+    step1()
     lcopy.wait()
     prep_a(0)
-    step1()
     prep_b(0)
+    step2()
     prep_a(1)
-    step2()
     prep_b(1)
+    step3()
     prep_a(2)
-    step3()
     prep_b(2)
+    step4()
     locals_[0].wait()
     swap.finish()
     synth(0)
-    step4()
+    step5()
     synth(1)
-    step5()
     synth(2)
+    step9()
+    synth(3)
     whole(0)
-    synth(3)
     whole(1)
+    synth(4)
     whole(2)
-    synth(4)
-    step9()
+    whole(3)
     locals_[1].wait()
     swap.sent()
     for copy in outs:
@@ -340,18 +336,17 @@
         first_kernel,
         out_shape=(jax.ShapeDtypeStruct((16, BLOCK, 128), F32), jax.ShapeDtypeStruct((5, 672, 640), F32),
                    jax.ShapeDtypeStruct((3, 384, 1280), BF)),
-        in_specs=[hbm, hbm, vm, vm, hbm],
+        in_specs=[hbm, vm, vm, vm, hbm],
         out_specs=(hbm, hbm, hbm),
         scratch_shapes=[
             pltpu.VMEM((8, 85, 384), F32),
-            pltpu.VMEM((85, 384), F32),
             pltpu.VMEM((3, 384, 640), F32),
             pltpu.VMEM((640, 640), BF),
             pltpu.VMEM((3, 640, 1152), BF),
             pltpu.VMEM((3, 384, 1280), BF),
             pltpu.VMEM((640, 1152), BF),
             pltpu.VMEM((5, 672, 640), F32),
-            dma((8,)), dma((8,)), dma((38,)), dma((38,)), dma((3,)), dma((8,)),
+            dma((7,)), dma((7,)), dma((38,)), dma((38,)), dma((3,)), dma((8,)),
         ],
         compiler_params=pltpu.CompilerParams(collective_id=0, has_side_effects=True, vmem_limit_bytes=58 * 2**20),
     )(spec, own, lat, w, leg)
@@ -481,16 +476,15 @@
     )(starts, wt, g, lp, cov)
 
 
-def return_kernel(src, dst, relay, a_send, a_recv, l_sem):
+def return_kernel(src, dst, a_send, a_recv, l_sem):
     me = lax.axis_index("lev")
     peers = lev_peers()
     greet(peers)
     met(peers)
-    swap = Exchange(src, dst, relay, a_send, a_recv)
+    swap = Exchange(src, dst, a_send, a_recv)
     swap.start()
     own = pltpu.make_async_copy(src.at[me], dst.at[me], l_sem)
     own.start()
-    swap.hand_on()
     own.wait()
     swap.finish()
     swap.sent()
@@ -498,13 +492,14 @@
 
 def give_back(x):
     hbm = pl.BlockSpec(memory_space=pl.ANY)
+    vm = pl.BlockSpec(memory_space=pltpu.VMEM)
     dma = pltpu.SemaphoreType.DMA
     return pl.pallas_call(
         return_kernel,
         out_shape=jax.ShapeDtypeStruct(x.shape, F32),
         in_specs=[hbm],
-        out_specs=hbm,
-        scratch_shapes=[pltpu.VMEM((85, 384), F32), dma((8,)), dma((8,)), dma(())],
+        out_specs=vm,
+        scratch_shapes=[dma((7,)), dma((7,)), dma(())],
         compiler_params=pltpu.CompilerParams(collective_id=1, has_side_effects=True),
     )(x)
 

time: 113 us -> 106 us (0.938); the launches traced: 112 us -> 106 us
  Pallas kernels: 102 us -> 96.4 us
    pallas_call x1, Pallas kernels: 21.5 us -> 16.7 us  [give_back(): pl.pallas_call(return_kernel, out_shape=jax.ShapeDtypeStruct(x.shape, F32...]
    pallas_call x1, Pallas kernels: 50.2 us -> 49.1 us  [first(): pl.pallas_call(first_kernel, out_shape=(jax.ShapeDtypeStruct((16, BLOCK,...]
where the time goes in v3:
time: 106 us
  Pallas kernels  96.4 us (91%)
  local copies, waits for them, and re-layouts  7.59 us (7%)
  other arithmetic  1.77 us (2%)
    pallas_call x1, Pallas kernels, first(): pl.pallas_call(first_kernel, out_shape=(jax.ShapeDtypeStruct((16, BLOCK,...  49.1 us
    pallas_call x1, Pallas kernels, second(): pl.pallas_call(second_kernel, out_shape=jax.ShapeDtypeStruct((8, 85, 384)...  30.6 us
    pallas_call x1, Pallas kernels, give_back(): pl.pallas_call(return_kernel, out_shape=jax.ShapeDtypeStruct(x.shape, F32...  16.7 us

profile of v3, /device:TPU:1, one launch (start us, length us, event | category | flops | bytes accessed | tf_op | source)
XLA Modules:
  0.0 105.9 jit_solution(9410414571426029830)
XLA Ops:
  0.0 1.3 %copy.32 = f32[4,2,136,136]{3,2,0,1:T(8,128)S(1)} copy(f32[4,2,136,136]{3,2,1,0:T(8,128)} %param.10) | data formatting | bytes 1183744 | tf_op args[4]
  1.5 0.0 copy-start.3
  1.5 0.0 copy-start.4
  1.5 0.3 copy.26
  1.8 0.1 copy.27
  1.9 0.1 pad.3.clone
  2.0 1.1 %maximum_maximum_fusion.own_ref = f32[1248,128]{1,0:T(8,128)} fusion(f32[136,64]{1,0:T(8,128)S(1)} %copy.27, f32[1088,128]{1,0:T(8,128)S(1)} %bitcast.19, f32[1248]{0:T(1024)S(1)} %pad.3.clone), kind=kLoop, calls=%fused_computation.1 | loop fusion | flops 479232 | bytes 1235840 | tf_op jit(solution)/shard_map/concatenate | solution.py:35
  3.1 0.0 copy-done.3
  3.1 0.1 copy.23
  3.2 0.0 copy-done.4
  3.3 0.1 copy.22
  3.4 0.0 copy-start
  3.4 0.7 copy.29.w
  4.1 0.0 copy-done.1
  4.1 0.1 copy.24
  4.2 0.0 copy-start.2
  4.2 1.2 %reshape.26.spec = f32[8,85,384]{2,1,0:T(8,128)} reshape(f32[20,2,17,384]{3,2,1,0:T(8,128)S(1)} %copy.24) | data formatting | bytes 2088960 | tf_op jit(solution)/shard_map/reshape | solution.py:509
  5.4 0.6 reshape.31.lat
  6.0 49.1 %shard_map.64 = (f32[16,1248,128]{2,1,0:T(8,128)}, f32[5,672,640]{2,1,0:T(8,128)}, bf16[3,384,1280]{2,1,0:T(8,128)(2,1)}) custom-call(f32[8,85,384]{2,1,0:T(8,128)} %reshape.26.spec, f32[1248,128]{1,0:T(8,128)} %maximum_maximum_fusion.own_ref, s32[1,640]{1,0:T(1,128)} %reshape.31.lat, f32[4,384]{1,0:T(4,128)} %copy.29.w, f32[20,384,640]{2,1,0:T(8,128)} %leg.1), custom_call_target="tpu_custom_call" | custom-call | tf_op jit(solution)/shard_map/pallas_call | solution.py:335
  55.0 0.6 convert_reduce_fusion.starts
  55.7 30.6 %shard_map.65.src = f32[8,85,384]{2,1,0:T(8,128)} custom-call(s32[40]{0:T(128)} %convert_reduce_fusion.starts, f32[384,4]{1,0:T(8,128)} %bitcast.21, f32[5,672,640]{2,1,0:T(8,128)} %get-tuple-element.8.g_hbm, bf16[3,384,1280]{2,1,0:T(8,128)(2,1)} %get-tuple-element.9.lp_hbm, f32[16,1248,128]{2,1,0:T(8,128)} %get-tuple-element.10.cov_hbm), custom_call_target="tpu_custom_call" | custom-call | tf_op jit(solution)/shard_map/pallas_call | solution.py:462
  86.3 16.7 %shard_map.66 = f32[8,85,384]{2,1,0:T(8,128)} custom-call(f32[8,85,384]{2,1,0:T(8,128)} %shard_map.65.src), custom_call_target="tpu_custom_call" | custom-call | tf_op jit(solution)/shard_map/pallas_call | solution.py:497
  103.0 1.4 %reshape.32 = f32[20,2,17,384]{3,2,1,0:T(8,128)S(1)} reshape(f32[8,85,384]{2,1,0:T(8,128)} %shard_map.66) | data formatting | bytes 2088960 | tf_op jit(solution)/shard_map/reshape | solution.py:513
  104.4 1.5 %copy.30 = f32[20,17,2,384]{3,2,1,0:T(2,128)} copy(f32[20,17,2,384]{3,1,2,0:T(8,128)S(1)} %bitcast.15) | data formatting | bytes 2088960 | tf_op jit(solution)/shard_map/transpose | solution.py:514
  (10 shorter events, 0.1 us)
Async XLA Ops:
  1.5 1.6 %copy-start.3 = (f32[4,384]{1,0:T(4,128)S(1)}, f32[4,384]{1,0:T(4,128)}, u32[]{:S(2)}) copy-start(f32[4,384]{1,0:T(4,128)} %param.7) | copy-start | bytes 18436
  1.5 1.7 %copy-start.4 = (s32[4,12]{1,0:T(4,128)S(1)}, s32[4,12]{1,0:T(4,128)}, u32[]{:S(2)}) copy-start(s32[4,12]{1,0:T(4,128)} %param.8) | copy-start | bytes 580
  1.8 2.3 %copy-start.1 = (f32[20,17,2,384]{3,2,1,0:T(2,128)S(1)}, f32[20,17,2,384]{3,2,1,0:T(2,128)}, u32[]{:S(2)}) copy-start(f32[20,17,2,384]{3,2,1,0:T(2,128)} %param.6) | copy-start | bytes 3133444
  3.4 0.8 copy-start
  4.2 1.2 %copy-start.2 = (s32[640]{0:T(1024)S(1)}, s32[640]{0:T(1024)}, u32[]{:S(2)}) copy-start(s32[640]{0:T(1024)} %param.11) | copy-start | bytes 7684

commit v4 on v3

--- a/solution.py
+++ b/solution.py
@@ -284,11 +284,12 @@
         s_cat[512:640, 768:1152] = hi
 
         def body(t, _):
-            off = pl.multiple_of(t * 128, 128)
-            g[s, 0:640, pl.ds(off, 128)] = dot_nt(a_cat[mi], s_cat[pl.ds(off, 128), :])
+            off = pl.multiple_of(t * 256, 256)
+            g[s, 0:640, pl.ds(off, 256)] = dot_nt(a_cat[mi], s_cat[pl.ds(off, 256), :])
             return 0
 
-        lax.fori_loop(0, 5, body, 0)
+        lax.fori_loop(0, 2, body, 0)
+        g[s, 0:640, 512:640] = dot_nt(a_cat[mi], s_cat[512:640, :])
         out(g.at[s], g_out.at[s], 3 + s)
 
     begin()
@@ -385,65 +386,81 @@
     lane128 = lax.broadcasted_iota(jnp.int32, (1, 128), 1)
     lane32 = lax.broadcasted_iota(jnp.int32, (1, 32), 1)
 
-    def covary(c, _):
-        lo_row, hi_row = starts[c], starts[c + 1]
-        base = (lo_row // 8) * 8
-        blk, odd = c // 2, lax.rem(c, 2)
-
-        @pl.when(odd == 0)
-        def _():
-            cov_copy(blk).wait()
-
-        top = HALF_BLOCK * odd
+    def side(c, blk, odd):
         u = cov[blk, 1088:1224, :]
         u = jnp.where(lax.rem(lane128 // 32, 2) == odd, u, pltpu.roll(u, 32, 1))
         u = jnp.concatenate([u[0:128], u[128:136], u[128:136], u[128:136], u[128:136]], axis=0)
         uhi, ulo = split(u)
-        ucat = jnp.where(lane128 < 64, uhi.astype(F32), ulo.astype(F32))
-        trow = cov[blk, pl.ds(pl.multiple_of(top + 512, 8), 32), :]
-
-        def window(t, _):
-            r0 = pl.multiple_of(base + 32 * t, 8)
-            x = jnp.concatenate([g[s, pl.ds(r0, 32), :] for s in range(5)], axis=0)
-            xhi, xlo = split(x)
-            t_hi, t_lo = xhi[:, 512:640].astype(F32), xlo[:, 512:640].astype(F32)
-            tcat = jnp.where((lane128 >= 32) & (lane128 < 64), t_lo, t_hi).astype(BF)
-            keep = r0 + lax.broadcasted_iota(jnp.int32, (32, 1), 0) >= lo_row
-            tail_out = jnp.zeros((160, 32), F32)
+        return jnp.where(lane128 < 64, uhi.astype(F32), ulo.astype(F32))
+
+    def window(c, blk, odd, ucat, r0, lo_row, hi_row):
+        top = HALF_BLOCK * odd
+        trow = cov[blk, top + 512:top + 544, :]
+        x = jnp.concatenate([g[s, pl.ds(r0, 32), :] for s in range(5)], axis=0)
+        xhi, xlo = split(x)
+        t_hi, t_lo = xhi[:, 512:640].astype(F32), xlo[:, 512:640].astype(F32)
+        tcat = jnp.where((lane128 >= 32) & (lane128 < 64), t_lo, t_hi).astype(BF)
+        row = r0 + lax.broadcasted_iota(jnp.int32, (32, 1), 0)
+        keep = (row >= lo_row) & (row < hi_row)
+        tail_out = jnp.zeros((160, 32), F32)
+        made = []
+        for b in range(4):
+            of_b = (lax.rem(lane128, 32) >= 8 * b) & (lax.rem(lane128, 32) < 8 * b + 8)
+            ub = jnp.where(of_b, ucat, 0.0).astype(BF)
+            chi, clo = split(jnp.concatenate([cov[blk, top + 128 * b:top + 128 * b + 128, :], trow], axis=0))
+            xb = xhi[:, 128 * b:128 * b + 128]
+            lhs = jnp.concatenate([xb, xlo[:, 128 * b:128 * b + 128], xb, tcat], axis=1)
+            rhs = jnp.concatenate([chi, chi, clo, ub], axis=1)
+            res = dot_nt(lhs, rhs)
+            made.append(res[:, 0:128])
+            tail_out = jnp.where((lane32 >= 8 * b) & (lane32 < 8 * b + 8), res[:, 128:160], tail_out)
+        return r0, keep, made, tail_out
+
+    def put(r0, keep, made, tail_out):
+        for s in range(5):
             for b in range(4):
-                of_b = (lax.rem(lane128, 32) >= 8 * b) & (lax.rem(lane128, 32) < 8 * b + 8)
-                ub = jnp.where(of_b, ucat, 0.0).astype(BF)
-                main = cov[blk, pl.ds(pl.multiple_of(top + 128 * b, 8), 128), :]
-                chi, clo = split(jnp.concatenate([main, trow], axis=0))
-                xb = xhi[:, 128 * b:128 * b + 128]
-                lhs = jnp.concatenate([xb, xlo[:, 128 * b:128 * b + 128], xb, tcat], axis=1)
-                rhs = jnp.concatenate([chi, chi, clo, ub], axis=1)
-                res = dot_nt(lhs, rhs)
-                for s in range(5):
-                    old = cv[s, pl.ds(r0, 32), 128 * b:128 * b + 128]
-                    cv[s, pl.ds(r0, 32), 128 * b:128 * b + 128] = jnp.where(keep, res[32 * s:32 * s + 32, 0:128], old)
-                tail_out = jnp.where((lane32 >= 8 * b) & (lane32 < 8 * b + 8), res[:, 128:160], tail_out)
-            for s in range(5):
-                old = cv[s, pl.ds(r0, 32), 512:544]
-                cv[s, pl.ds(r0, 32), 512:544] = jnp.where(keep, tail_out[32 * s:32 * s + 32], old)
-            return 0
-
-        lax.fori_loop(0, (hi_row - base + 31) // 32, window, 0)
+                old = cv[s, pl.ds(r0, 32), 128 * b:128 * b + 128]
+                cv[s, pl.ds(r0, 32), 128 * b:128 * b + 128] = jnp.where(keep, made[b][32 * s:32 * s + 32], old)
+            old = cv[s, pl.ds(r0, 32), 512:544]
+            cv[s, pl.ds(r0, 32), 512:544] = jnp.where(keep, tail_out[32 * s:32 * s + 32], old)
+
+    def covary(blk, _):
+        cov_copy(blk).wait()
+        firsts = []
+        for odd in range(2):
+            c = 2 * blk + odd
+            lo_row, hi_row = starts[c], starts[c + 1]
+            base = jnp.minimum((lo_row // 8) * 8, 632)
+            ucat = side(c, blk, odd)
+            firsts.append(window(c, blk, odd, ucat, pl.multiple_of(base, 8), lo_row, hi_row))
+        for one in firsts:
+            put(*one)
+        for odd in range(2):
+            c = 2 * blk + odd
+            lo_row, hi_row = starts[c], starts[c + 1]
+            base = jnp.minimum((lo_row // 8) * 8, 632)
+
+            def more(t, _):
+                put(*window(c, blk, odd, side(c, blk, odd), pl.multiple_of(base + 32 * t, 8), lo_row, hi_row))
+                return 0
+
+            lax.fori_loop(1, (hi_row - base + 31) // 32, more, 0)
         return 0
 
-    lax.fori_loop(0, 32, covary, 0)
+    lax.fori_loop(0, 16, covary, 0)
     for copy in lcopies:
         copy.wait()
 
     for s in range(5):
         mi = (s + o) // 2
         acc = None
-        for b in range(5):
-            hi, lo = split(cv[s, 0:640, 128 * b:128 * b + 128])
+        for b, wide in ((0, 256), (256, 256), (512, 128)):
+            hi, lo = split(cv[s, 0:640, b:b + wide])
             rhs = jnp.concatenate([hi, lo, hi], axis=0)
             one = jnp.dot(lp_cat[mi], rhs, preferred_element_type=F32)
-            one = one * wcol[:, 128 * b:128 * b + 128]
-            if b < 4:
+            one = one * wcol[:, b:b + wide]
+            if b < 512:
+                one = one[:, 0:128] + one[:, 128:256]
                 acc = one if acc is None else acc + one
             else:
                 tail = one

time: 106 us -> 95.6 us (0.902)
  Pallas kernels: 96.4 us -> 85.9 us
    pallas_call x1, Pallas kernels: 30.6 us -> 23 us  [second(): pl.pallas_call(second_kernel, out_shape=jax.ShapeDtypeStruct((8, 85, 384)...]
    pallas_call x1, Pallas kernels: 49.1 us -> 46.2 us  [first(): pl.pallas_call(first_kernel, out_shape=(jax.ShapeDtypeStruct((16, BLOCK,...]
where the time goes in v4:
time: 95.6 us; the launch traced here: 95.4 us
  Pallas kernels  85.9 us (90%)
  local copies, waits for them, and re-layouts  7.59 us (8%)
  other arithmetic  1.77 us (2%)
    pallas_call x1, Pallas kernels, first(): pl.pallas_call(first_kernel, out_shape=(jax.ShapeDtypeStruct((16, BLOCK,...  46.2 us
    pallas_call x1, Pallas kernels, second(): pl.pallas_call(second_kernel, out_shape=jax.ShapeDtypeStruct((8, 85, 384)...  23 us
    pallas_call x1, Pallas kernels, give_back(): pl.pallas_call(return_kernel, out_shape=jax.ShapeDtypeStruct(x.shape, F32...  16.7 us

profile of v4, /device:TPU:1, one launch (start us, length us, event | category | flops | bytes accessed | tf_op | source)
XLA Modules:
  0.0 95.4 jit_solution(12824661508545141370)
XLA Ops:
  0.0 1.3 %copy.32 = f32[4,2,136,136]{3,2,0,1:T(8,128)S(1)} copy(f32[4,2,136,136]{3,2,1,0:T(8,128)} %param.10) | data formatting | bytes 1183744 | tf_op args[4]
  1.5 0.0 copy-start.3
  1.5 0.0 copy-start.4
  1.5 0.3 copy.26
  1.8 0.1 copy.27
  1.9 0.1 pad.3.clone
  2.0 1.1 %maximum_maximum_fusion.own_ref = f32[1248,128]{1,0:T(8,128)} fusion(f32[136,64]{1,0:T(8,128)S(1)} %copy.27, f32[1088,128]{1,0:T(8,128)S(1)} %bitcast.19, f32[1248]{0:T(1024)S(1)} %pad.3.clone), kind=kLoop, calls=%fused_computation.1 | loop fusion | flops 479232 | bytes 1235840 | tf_op jit(solution)/shard_map/concatenate | solution.py:35
  3.1 0.0 copy-done.3
  3.1 0.1 copy.23
  3.2 0.0 copy-done.4
  3.3 0.1 copy.22
  3.4 0.0 copy-start
  3.4 0.7 copy.29.w
  4.1 0.0 copy-done.1
  4.1 0.1 copy.24
  4.2 0.0 copy-start.2
  4.2 1.2 %reshape.26.spec = f32[8,85,384]{2,1,0:T(8,128)} reshape(f32[20,2,17,384]{3,2,1,0:T(8,128)S(1)} %copy.24) | data formatting | bytes 2088960 | tf_op jit(solution)/shard_map/reshape | solution.py:526
  5.4 0.6 reshape.31.lat
  6.0 46.2 %shard_map.64 = (f32[16,1248,128]{2,1,0:T(8,128)}, f32[5,672,640]{2,1,0:T(8,128)}, bf16[3,384,1280]{2,1,0:T(8,128)(2,1)}) custom-call(f32[8,85,384]{2,1,0:T(8,128)} %reshape.26.spec, f32[1248,128]{1,0:T(8,128)} %maximum_maximum_fusion.own_ref, s32[1,640]{1,0:T(1,128)} %reshape.31.lat, f32[4,384]{1,0:T(4,128)} %copy.29.w, f32[20,384,640]{2,1,0:T(8,128)} %leg.1), custom_call_target="tpu_custom_call" | custom-call | tf_op jit(solution)/shard_map/pallas_call | solution.py:336
  52.2 0.6 convert_reduce_fusion.starts
  52.8 23.0 %shard_map.65.src = f32[8,85,384]{2,1,0:T(8,128)} custom-call(s32[40]{0:T(128)} %convert_reduce_fusion.starts, f32[384,4]{1,0:T(8,128)} %bitcast.21, f32[5,672,640]{2,1,0:T(8,128)} %get-tuple-element.8.g_hbm, bf16[3,384,1280]{2,1,0:T(8,128)(2,1)} %get-tuple-element.9.lp_hbm, f32[16,1248,128]{2,1,0:T(8,128)} %get-tuple-element.10.cov_hbm), custom_call_target="tpu_custom_call" | custom-call | tf_op jit(solution)/shard_map/pallas_call | solution.py:479
  75.8 16.7 %shard_map.66 = f32[8,85,384]{2,1,0:T(8,128)} custom-call(f32[8,85,384]{2,1,0:T(8,128)} %shard_map.65.src), custom_call_target="tpu_custom_call" | custom-call | tf_op jit(solution)/shard_map/pallas_call | solution.py:514
  92.5 1.4 %reshape.32 = f32[20,2,17,384]{3,2,1,0:T(8,128)S(1)} reshape(f32[8,85,384]{2,1,0:T(8,128)} %shard_map.66) | data formatting | bytes 2088960 | tf_op jit(solution)/shard_map/reshape | solution.py:530
  93.9 1.5 %copy.30 = f32[20,17,2,384]{3,2,1,0:T(2,128)} copy(f32[20,17,2,384]{3,1,2,0:T(8,128)S(1)} %bitcast.15) | data formatting | bytes 2088960 | tf_op jit(solution)/shard_map/transpose | solution.py:531
  (10 shorter events, 0.1 us)
Async XLA Ops:
  1.5 1.6 %copy-start.3 = (f32[4,384]{1,0:T(4,128)S(1)}, f32[4,384]{1,0:T(4,128)}, u32[]{:S(2)}) copy-start(f32[4,384]{1,0:T(4,128)} %param.7) | copy-start | bytes 18436
  1.5 1.7 %copy-start.4 = (s32[4,12]{1,0:T(4,128)S(1)}, s32[4,12]{1,0:T(4,128)}, u32[]{:S(2)}) copy-start(s32[4,12]{1,0:T(4,128)} %param.8) | copy-start | bytes 580
  1.8 2.3 %copy-start.1 = (f32[20,17,2,384]{3,2,1,0:T(2,128)S(1)}, f32[20,17,2,384]{3,2,1,0:T(2,128)}, u32[]{:S(2)}) copy-start(f32[20,17,2,384]{3,2,1,0:T(2,128)} %param.6) | copy-start | bytes 3133444
  3.4 0.8 copy-start
  4.2 1.2 %copy-start.2 = (s32[640]{0:T(1024)S(1)}, s32[640]{0:T(1024)}, u32[]{:S(2)}) copy-start(s32[640]{0:T(1024)} %param.11) | copy-start | bytes 7684

commit v5 on v4

--- a/solution.py
+++ b/solution.py
@@ -25,14 +25,18 @@
     return lax.dot_general(a, b, NT, preferred_element_type=F32)
 
 
-def pack_cov(vc):
-    t = jnp.transpose(vc, (1, 0, 2, 3))
-    main = t[:, :, :128, :128].reshape(2, 512, 128)
-    rows = t[:, :, 128:, :128].reshape(2, 32, 128)
-    u = jnp.transpose(t[:, :, :, 128:], (2, 0, 1, 3)).reshape(136, 64)
-    u = jnp.concatenate([u, u], axis=1)
-    top = jnp.concatenate([main, rows], axis=1).reshape(2 * HALF_BLOCK, 128)
-    return jnp.concatenate([top, u, jnp.zeros((BLOCK - 1224, 128), F32)], axis=0)
+def pack_cov(vc, side, own):
+    side[...] = jnp.zeros((136, 128), F32)
+    u = jnp.zeros((136, 128), F32)
+    for c in range(2):
+        for b in range(4):
+            own[HALF_BLOCK * c + 128 * b:HALF_BLOCK * c + 128 * b + 128, :] = vc[b, c, 0:128, 0:128]
+            own[HALF_BLOCK * c + 512 + 8 * b:HALF_BLOCK * c + 520 + 8 * b, :] = vc[b, c, 128:136, 0:128]
+            side[:, 0:8] = vc[b, c, :, 128:136]
+            at_lane = 32 * c + 8 * b
+            u = u + (pltpu.roll(side[...], at_lane, 1) if at_lane else side[...])
+    own[1088:1224, :] = u + pltpu.roll(u, 64, 1)
+    own[1224:BLOCK, :] = jnp.zeros((BLOCK - 1224, 128), F32)
 
 
 def place():
@@ -90,8 +94,8 @@
     return m0, o, lax.axis_index("wave") * 20 + m0
 
 
-def first_kernel(spec, own_ref, lat, w, leg, cov_out, g_out, lp_out,
-                 s_in, lbuf, perm, a_cat, lp, s_cat, g,
+def first_kernel(spec, vc, lat, band_filter, band_blocks, leg, cov_out, g_out, lp_out,
+                 own_ref, side, w, s_in, lbuf, perm, a_cat, lp, s_cat, g,
                  a_send, a_recv, c_send, c_recv, l_sem, o_sem):
     z, xh, core, y, xl = place()
     me = lax.axis_index("lev")
@@ -106,6 +110,12 @@
     greet(peers)
     lcopy = pltpu.make_async_copy(leg.at[pl.ds(m0, 3)], lbuf, l_sem.at[0])
     lcopy.start()
+    pack_cov(vc, side, own_ref)
+    keep = jnp.zeros((4, 384), F32)
+    block_of = lax.broadcasted_iota(jnp.int32, (4, 384), 1) // 32
+    for n in range(12):
+        keep = jnp.where(block_of == n, band_blocks[:, n:n + 1].astype(F32), keep)
+    w[...] = band_filter[...] * keep
 
     def block(zz, xx, kk=None):
         return (zz * 2 + xx) * 2 + (core if kk is None else kk)
@@ -238,7 +248,7 @@
     def order():
         for s in range(5):
             g[s, 640:672, :] = jnp.zeros((32, 640), F32)
-        row = jnp.broadcast_to(lat[...], (8, 640)).astype(F32)
+        row = jnp.broadcast_to(lat[...].reshape(1, 640), (8, 640)).astype(F32)
         column = row.T[:, 0:1]
         mine = row[0:1]
         p_row = lax.broadcasted_iota(jnp.int32, (1, 640), 1)
@@ -329,7 +339,7 @@
         copy.wait_send()
 
 
-def first(spec, own, lat, w, leg):
+def first(spec, vc, lat, band_filter, band_blocks, leg):
     hbm = pl.BlockSpec(memory_space=pl.ANY)
     vm = pl.BlockSpec(memory_space=pltpu.VMEM)
     dma = pltpu.SemaphoreType.DMA
@@ -337,9 +347,12 @@
         first_kernel,
         out_shape=(jax.ShapeDtypeStruct((16, BLOCK, 128), F32), jax.ShapeDtypeStruct((5, 672, 640), F32),
                    jax.ShapeDtypeStruct((3, 384, 1280), BF)),
-        in_specs=[hbm, vm, vm, vm, hbm],
+        in_specs=[hbm, vm, vm, vm, vm, hbm],
         out_specs=(hbm, hbm, hbm),
         scratch_shapes=[
+            pltpu.VMEM((BLOCK, 128), F32),
+            pltpu.VMEM((136, 128), F32),
+            pltpu.VMEM((4, 384), F32),
             pltpu.VMEM((8, 85, 384), F32),
             pltpu.VMEM((3, 384, 640), F32),
             pltpu.VMEM((640, 640), BF),
@@ -350,7 +363,7 @@
             dma((7,)), dma((7,)), dma((38,)), dma((38,)), dma((3,)), dma((8,)),
         ],
         compiler_params=pltpu.CompilerParams(collective_id=0, has_side_effects=True, vmem_limit_bytes=58 * 2**20),
-    )(spec, own, lat, w, leg)
+    )(spec, vc, lat, band_filter, band_blocks, leg)
 
 
 def second_kernel(starts, wt, g_hbm, lp_hbm, cov_hbm, out_ref, cov, lp_cat, g, cv, wcol, gsem, lsem, csem):
@@ -493,7 +506,7 @@
     )(starts, wt, g, lp, cov)
 
 
-def return_kernel(src, dst, a_send, a_recv, l_sem):
+def return_kernel(src, out, dst, a_send, a_recv, l_sem):
     me = lax.axis_index("lev")
     peers = lev_peers()
     greet(peers)
@@ -504,6 +517,9 @@
     own.start()
     own.wait()
     swap.finish()
+    for j in range(8):
+        for s in range(5):
+            out[5 * j + s] = dst[j, 17 * s:17 * s + 17, :]
     swap.sent()
 
 
@@ -513,10 +529,10 @@
     dma = pltpu.SemaphoreType.DMA
     return pl.pallas_call(
         return_kernel,
-        out_shape=jax.ShapeDtypeStruct(x.shape, F32),
+        out_shape=jax.ShapeDtypeStruct((40, 17, 384), F32),
         in_specs=[hbm],
         out_specs=vm,
-        scratch_shapes=[dma((7,)), dma((7,)), dma(())],
+        scratch_shapes=[pltpu.VMEM(x.shape, F32), dma((7,)), dma((7,)), dma(())],
         compiler_params=pltpu.CompilerParams(collective_id=1, has_side_effects=True),
     )(x)
 
@@ -524,7 +540,7 @@
 def local(spectra, band_filter, band_blocks, legendre, vert_cov, lat_cov):
     w = band_filter * jnp.repeat(band_blocks.astype(F32), 32, axis=1)
     spec = jnp.transpose(spectra, (0, 2, 1, 3)).reshape(8, 85, 384)
-    cov, g, lp = first(spec, pack_cov(vert_cov), lat_cov.reshape(1, 640), w, legendre)
+    cov, g, lp = first(spec, vert_cov, lat_cov, band_filter, band_blocks, legendre)
     bounds = jnp.arange(40, dtype=jnp.int32)
     starts = jnp.sum((lat_cov[:, None] < bounds[None, :]).astype(jnp.int32), axis=0)
     back = give_back(second(starts, w.T, g, lp, cov)).reshape(20, 2, 17, 384)

time: 95.6 us -> 93.1 us (0.974)
  local copies, waits for them, and re-layouts: 7.59 us -> 5.65 us
    transpose x3 -> x0, local copies, waits for them, and re-layouts: 1.83 us -> none  [the longest x1 1.5 us: local(): return jnp.transpose(back, (0, 2, 1, 3))]
    reshape x1, local copies, waits for them, and re-layouts: 1.38 us -> 2.87 us  [local(): back = give_back(second(starts, w.T, g, lp, cov)).reshape(20, 2, 17, 384)]
    unnamed x12 -> x7, local copies, waits for them, and re-layouts: 1.5 us -> 0.15 us
    transpose x1, local copies, waits for them, and re-layouts: 0.12 us -> 1.34 us  [local(): spec = jnp.transpose(spectra, (0, 2, 1, 3)).reshape(8, 85, 384)]
    concatenate x2 -> x0, other arithmetic: 1.12 us -> none  [the longest x1 1.08 us: pack_cov(): jnp.concatenate([top, u, jnp.zeros((BLOCK - 1224, 128), F32)], axis=0)]
where the time goes in v5:
time: 93.1 us; the launch traced here: 92.8 us
  Pallas kernels  85.8 us (92%)
  local copies, waits for them, and re-layouts  5.65 us (6%)
  other arithmetic  1.35 us (1%)
    pallas_call x1, Pallas kernels, first(): pl.pallas_call(first_kernel, out_shape=(jax.ShapeDtypeStruct((16, BLOCK,...  46.4 us
    pallas_call x1, Pallas kernels, second(): pl.pallas_call(second_kernel, out_shape=jax.ShapeDtypeStruct((8, 85, 384)...  22.4 us
    pallas_call x1, Pallas kernels, give_back(): pl.pallas_call(return_kernel, out_shape=jax.ShapeDtypeStruct((40, 17, 384...  17 us
    reshape x1, local copies, waits for them, and re-layouts, local(): back = give_back(second(starts, w.T, g, lp, cov)).reshape(20, 2, 17, 384)  2.87 us

profile of v5, /device:TPU:1, one launch (start us, length us, event | category | flops | bytes accessed | tf_op | source)
XLA Modules:
  0.0 92.8 jit_solution(2845609178512308571)
XLA Ops:
  0.0 1.3 %copy.17 = f32[20,2,17,384]{3,2,1,0:T(8,128)S(1)} copy(f32[20,2,17,384]{3,1,2,0:T(2,128)} %bitcast.9) | data formatting | bytes 2088960 | tf_op jit(solution)/shard_map/transpose | solution.py:542
  1.3 1.2 %reshape.11.spec = f32[8,85,384]{2,1,0:T(8,128)} reshape(f32[20,2,17,384]{3,2,1,0:T(8,128)S(1)} %copy.17) | data formatting | bytes 2088960 | tf_op jit(solution)/shard_map/reshape | solution.py:542
  2.5 0.0 copy-start
  2.5 0.0 copy-start.2
  2.5 0.0 copy-start.1
  2.5 46.4 %shard_map.64 = (f32[16,1248,128]{2,1,0:T(8,128)}, f32[5,672,640]{2,1,0:T(8,128)}, bf16[3,384,1280]{2,1,0:T(8,128)(2,1)}) custom-call(f32[8,85,384]{2,1,0:T(8,128)} %reshape.11.spec, f32[4,2,136,136]{3,2,1,0:T(8,128)} %vc.1, s32[640]{0:T(1024)} %lat.1, f32[4,384]{1,0:T(4,128)} %band_filter.1, s32[4,12]{1,0:T(4,128)} %band_blocks.1, f32[20,384,640]{2,1,0:T(8,128)} %leg.1), custom_call_target="tpu_custom_call" | custom-call | tf_op jit(solution)/shard_map/pallas_call | solution.py:346
  49.0 0.0 copy-done
  49.0 0.1 copy.16
  49.2 0.0 copy-done.2
  49.2 0.1 copy.15
  49.3 0.7 bitcast_multiply_fusion
  50.0 0.0 copy-done.1
  50.0 0.7 convert_reduce_fusion.starts
  50.6 22.4 %shard_map.65.src = f32[8,85,384]{2,1,0:T(8,128)} custom-call(s32[40]{0:T(128)} %convert_reduce_fusion.starts, f32[384,4]{1,0:T(8,128)} %bitcast.10, f32[5,672,640]{2,1,0:T(8,128)} %get-tuple-element.8.g_hbm, bf16[3,384,1280]{2,1,0:T(8,128)(2,1)} %get-tuple-element.9.lp_hbm, f32[16,1248,128]{2,1,0:T(8,128)} %get-tuple-element.10.cov_hbm), custom_call_target="tpu_custom_call" | custom-call | tf_op jit(solution)/shard_map/pallas_call | solution.py:492
  73.0 17.0 %shard_map.66 = f32[40,17,384]{2,1,0:T(8,128)} custom-call(f32[8,85,384]{2,1,0:T(8,128)} %shard_map.65.src), custom_call_target="tpu_custom_call" | custom-call | tf_op jit(solution)/shard_map/pallas_call | solution.py:530
  90.0 2.9 %copy.20 = f32[20,2,17,384]{3,1,2,0:T(2,128)} copy(f32[20,2,17,384]{3,2,1,0:T(8,128)} %bitcast.8) | data formatting | bytes 2088960 | tf_op jit(solution)/shard_map/reshape | solution.py:546
  (1 shorter events, 0.0 us)
Async XLA Ops:
  2.5 46.5 %copy-start = (f32[4,384]{1,0:T(4,128)S(1)}, f32[4,384]{1,0:T(4,128)}, u32[]{:S(2)}) copy-start(f32[4,384]{1,0:T(4,128)} %band_filter.1) | copy-start | bytes 18436
  2.5 46.6 %copy-start.2 = (s32[4,12]{1,0:T(4,128)S(1)}, s32[4,12]{1,0:T(4,128)}, u32[]{:S(2)}) copy-start(s32[4,12]{1,0:T(4,128)} %band_blocks.1) | copy-start | bytes 580
  2.5 47.4 %copy-start.1 = (s32[640]{0:T(1024)S(1)}, s32[640]{0:T(1024)}, u32[]{:S(2)}) copy-start(s32[640]{0:T(1024)} %lat.1) | copy-start | bytes 7684

commit v6 on v5

--- a/solution.py
+++ b/solution.py
@@ -92,6 +92,14 @@
     o = lax.rem(lev, 2)
     m0 = 5 * (lev // 2) + 2 * o
     return m0, o, lax.axis_index("wave") * 20 + m0
+
+
+def band_weights(band_filter, band_blocks):
+    keep = jnp.zeros((4, 384), F32)
+    block_of = lax.broadcasted_iota(jnp.int32, (4, 384), 1) // 32
+    for n in range(12):
+        keep = jnp.where(block_of == n, band_blocks[:, n:n + 1].astype(F32), keep)
+    return band_filter[...] * keep
 
 
 def first_kernel(spec, vc, lat, band_filter, band_blocks, leg, cov_out, g_out, lp_out,
@@ -111,11 +119,7 @@
     lcopy = pltpu.make_async_copy(leg.at[pl.ds(m0, 3)], lbuf, l_sem.at[0])
     lcopy.start()
     pack_cov(vc, side, own_ref)
-    keep = jnp.zeros((4, 384), F32)
-    block_of = lax.broadcasted_iota(jnp.int32, (4, 384), 1) // 32
-    for n in range(12):
-        keep = jnp.where(block_of == n, band_blocks[:, n:n + 1].astype(F32), keep)
-    w[...] = band_filter[...] * keep
+    w[...] = band_weights(band_filter, band_blocks)
 
     def block(zz, xx, kk=None):
         return (zz * 2 + xx) * 2 + (core if kk is None else kk)
@@ -307,12 +311,12 @@
     step1()
     lcopy.wait()
     prep_a(0)
+    prep_a(1)
+    step2()
+    prep_a(2)
     prep_b(0)
-    step2()
-    prep_a(1)
+    step3()
     prep_b(1)
-    step3()
-    prep_a(2)
     prep_b(2)
     step4()
     locals_[0].wait()
@@ -321,8 +325,8 @@
     step5()
     synth(1)
     synth(2)
+    synth(3)
     step9()
-    synth(3)
     whole(0)
     whole(1)
     synth(4)
@@ -366,7 +370,7 @@
     )(spec, vc, lat, band_filter, band_blocks, leg)
 
 
-def second_kernel(starts, wt, g_hbm, lp_hbm, cov_hbm, out_ref, cov, lp_cat, g, cv, wcol, gsem, lsem, csem):
+def second_kernel(starts, band_filter, band_blocks, g_hbm, lp_hbm, cov_hbm, out_ref, cov, lp_cat, g, cv, wcol, gsem, lsem, csem):
     m0, o, first_m = part()
     gcopies = [pltpu.make_async_copy(g_hbm.at[s], g.at[s], gsem.at[s]) for s in range(5)]
     for copy in gcopies:
@@ -384,6 +388,8 @@
                for n, (src, dst) in enumerate(((0, 0), (0, 640), (640, 1280)))]
     for copy in lcopies:
         copy.start()
+    w = band_weights(band_filter, band_blocks)
+    wt = jnp.concatenate([w, w], axis=0).T
     for b in range(4):
         wcol[:, 128 * b:128 * (b + 1)] = jnp.broadcast_to(wt[:, b:b + 1], (384, 128))
     lane = lax.broadcasted_iota(jnp.int32, (384, 128), 1)
@@ -485,14 +491,14 @@
             out_ref[j, 17 * s:17 * s + 17, :] = res[17 * j:17 * j + 17]
 
 
-def second(starts, wt, g, lp, cov):
+def second(starts, band_filter, band_blocks, g, lp, cov):
     hbm = pl.BlockSpec(memory_space=pl.ANY)
     vm = pl.BlockSpec(memory_space=pltpu.VMEM)
     dma = pltpu.SemaphoreType.DMA
     return pl.pallas_call(
         second_kernel,
         out_shape=jax.ShapeDtypeStruct((8, 85, 384), F32),
-        in_specs=[pl.BlockSpec(memory_space=pltpu.SMEM), vm, hbm, hbm, hbm],
+        in_specs=[pl.BlockSpec(memory_space=pltpu.SMEM), vm, vm, hbm, hbm, hbm],
         out_specs=vm,
         scratch_shapes=[
             pltpu.VMEM((16, BLOCK, 128), F32),
@@ -503,7 +509,7 @@
             dma((5,)), dma((3,)), dma((16,)),
         ],
         compiler_params=pltpu.CompilerParams(vmem_limit_bytes=58 * 2**20),
-    )(starts, wt, g, lp, cov)
+    )(starts, band_filter, band_blocks, g, lp, cov)
 
 
 def return_kernel(src, out, dst, a_send, a_recv, l_sem):
@@ -538,12 +544,11 @@
 
 
 def local(spectra, band_filter, band_blocks, legendre, vert_cov, lat_cov):
-    w = band_filter * jnp.repeat(band_blocks.astype(F32), 32, axis=1)
     spec = jnp.transpose(spectra, (0, 2, 1, 3)).reshape(8, 85, 384)
     cov, g, lp = first(spec, vert_cov, lat_cov, band_filter, band_blocks, legendre)
     bounds = jnp.arange(40, dtype=jnp.int32)
     starts = jnp.sum((lat_cov[:, None] < bounds[None, :]).astype(jnp.int32), axis=0)
-    back = give_back(second(starts, w.T, g, lp, cov)).reshape(20, 2, 17, 384)
+    back = give_back(second(starts, band_filter, band_blocks, g, lp, cov)).reshape(20, 2, 17, 384)
     return jnp.transpose(back, (0, 2, 1, 3))
 
 

time: 93.1 us -> 91.5 us (0.983)
    pallas_call x1, Pallas kernels: 46.4 us -> 45.1 us  [first(): pl.pallas_call(first_kernel, out_shape=(jax.ShapeDtypeStruct((16, BLOCK,...]
where the time goes in v6:
time: 91.5 us; the launch traced here: 91.2 us
  Pallas kernels  85.2 us (93%)
  local copies, waits for them, and re-layouts  5.41 us (6%)
    pallas_call x1, Pallas kernels, first(): pl.pallas_call(first_kernel, out_shape=(jax.ShapeDtypeStruct((16, BLOCK,...  45.1 us
    pallas_call x1, Pallas kernels, second(): pl.pallas_call(second_kernel, out_shape=jax.ShapeDtypeStruct((8, 85, 384)...  23 us
    pallas_call x1, Pallas kernels, give_back(): pl.pallas_call(return_kernel, out_shape=jax.ShapeDtypeStruct((40, 17, 384...  17 us
    reshape x1, local copies, waits for them, and re-layouts, local(): give_back(second(starts, band_filter, band_blocks, g, lp, cov))  2.87 us

profile of v6, /device:TPU:1, one launch (start us, length us, event | category | flops | bytes accessed | tf_op | source)
XLA Modules:
  0.0 91.2 jit_solution(13781327619040875948)
XLA Ops:
  0.0 1.3 %copy.11 = f32[20,2,17,384]{3,2,1,0:T(8,128)S(1)} copy(f32[20,2,17,384]{3,1,2,0:T(2,128)} %bitcast.6) | data formatting | bytes 2088960 | tf_op jit(solution)/shard_map/transpose | solution.py:547
  1.3 1.2 %reshape.7.spec = f32[8,85,384]{2,1,0:T(8,128)} reshape(f32[20,2,17,384]{3,2,1,0:T(8,128)S(1)} %copy.11) | data formatting | bytes 2088960 | tf_op jit(solution)/shard_map/reshape | solution.py:547
  2.5 0.0 copy-start
  2.5 45.1 %shard_map.64 = (f32[16,1248,128]{2,1,0:T(8,128)}, f32[5,672,640]{2,1,0:T(8,128)}, bf16[3,384,1280]{2,1,0:T(8,128)(2,1)}) custom-call(f32[8,85,384]{2,1,0:T(8,128)} %reshape.7.spec, f32[4,2,136,136]{3,2,1,0:T(8,128)} %vc.1, s32[640]{0:T(1024)} %lat.1, f32[4,384]{1,0:T(4,128)} %band_filter.3, s32[4,12]{1,0:T(4,128)} %band_blocks.3, f32[20,384,640]{2,1,0:T(8,128)} %leg.1), custom_call_target="tpu_custom_call" | custom-call | tf_op jit(solution)/shard_map/pallas_call | solution.py:350
  47.7 0.0 copy-done
  47.7 0.6 convert_reduce_fusion.starts
  48.3 23.0 %shard_map.65.src = f32[8,85,384]{2,1,0:T(8,128)} custom-call(s32[40]{0:T(128)} %convert_reduce_fusion.starts, f32[4,384]{1,0:T(4,128)} %band_filter.3, s32[4,12]{1,0:T(4,128)} %band_blocks.3, f32[5,672,640]{2,1,0:T(8,128)} %get-tuple-element.8.g_hbm, bf16[3,384,1280]{2,1,0:T(8,128)(2,1)} %get-tuple-element.9.lp_hbm, f32[16,1248,128]{2,1,0:T(8,128)} %get-tuple-element.10.cov_hbm), custom_call_target="tpu_custom_call" | custom-call | tf_op jit(solution)/shard_map/pallas_call | solution.py:498
  71.4 17.0 %shard_map.66 = f32[40,17,384]{2,1,0:T(8,128)} custom-call(f32[8,85,384]{2,1,0:T(8,128)} %shard_map.65.src), custom_call_target="tpu_custom_call" | custom-call | tf_op jit(solution)/shard_map/pallas_call | solution.py:536
  88.4 2.9 %copy.14 = f32[20,2,17,384]{3,1,2,0:T(2,128)} copy(f32[20,2,17,384]{3,2,1,0:T(8,128)} %bitcast.5) | data formatting | bytes 2088960 | tf_op jit(solution)/shard_map/reshape | solution.py:551
Async XLA Ops:
  2.5 45.2 %copy-start = (s32[640]{0:T(1024)S(1)}, s32[640]{0:T(1024)}, u32[]{:S(2)}) copy-start(s32[640]{0:T(1024)} %lat.1) | copy-start | bytes 7684

commit v7 on v6

--- a/solution.py
+++ b/solution.py
@@ -383,11 +383,9 @@
         cov_copy(n).start()
         return 0
 
-    lax.fori_loop(0, 16, begin, 0)
+    lax.fori_loop(0, 2, begin, 0)
     lcopies = [pltpu.make_async_copy(lp_hbm.at[:, :, pl.ds(src, 640)], lp_cat.at[:, :, pl.ds(dst, 640)], lsem.at[n])
                for n, (src, dst) in enumerate(((0, 0), (0, 640), (640, 1280)))]
-    for copy in lcopies:
-        copy.start()
     w = band_weights(band_filter, band_blocks)
     wt = jnp.concatenate([w, w], axis=0).T
     for b in range(4):
@@ -401,6 +399,9 @@
         cv[s, :, 512:640] = jnp.zeros((672, 128), F32)
     for copy in gcopies:
         copy.wait()
+    lax.fori_loop(2, 16, begin, 0)
+    for copy in lcopies:
+        copy.start()
 
     lane128 = lax.broadcasted_iota(jnp.int32, (1, 128), 1)
     lane32 = lax.broadcasted_iota(jnp.int32, (1, 32), 1)

time: 91.5 us -> 90.9 us (level)
  no operation moved by 1% of the time
where the time goes in v7:
time: 90.9 us
  Pallas kernels  84.8 us (93%)
  local copies, waits for them, and re-layouts  5.41 us (6%)
    pallas_call x1, Pallas kernels, first(): pl.pallas_call(first_kernel, out_shape=(jax.ShapeDtypeStruct((16, BLOCK,...  45.1 us
    pallas_call x1, Pallas kernels, second(): pl.pallas_call(second_kernel, out_shape=jax.ShapeDtypeStruct((8, 85, 384)...  22.6 us
    pallas_call x1, Pallas kernels, give_back(): pl.pallas_call(return_kernel, out_shape=jax.ShapeDtypeStruct((40, 17, 384...  17 us
    reshape x1, local copies, waits for them, and re-layouts, local(): give_back(second(starts, band_filter, band_blocks, g, lp, cov))  2.87 us

profile of v7, /device:TPU:1, one launch (start us, length us, event | category | flops | bytes accessed | tf_op | source)
XLA Modules:
  0.0 90.9 jit_solution(8246434883495418142)
XLA Ops:
  0.0 1.3 %copy.11 = f32[20,2,17,384]{3,2,1,0:T(8,128)S(1)} copy(f32[20,2,17,384]{3,1,2,0:T(2,128)} %bitcast.6) | data formatting | bytes 2088960 | tf_op jit(solution)/shard_map/transpose | solution.py:548
  1.3 1.2 %reshape.7.spec = f32[8,85,384]{2,1,0:T(8,128)} reshape(f32[20,2,17,384]{3,2,1,0:T(8,128)S(1)} %copy.11) | data formatting | bytes 2088960 | tf_op jit(solution)/shard_map/reshape | solution.py:548
  2.5 0.0 copy-start
  2.5 45.1 %shard_map.64 = (f32[16,1248,128]{2,1,0:T(8,128)}, f32[5,672,640]{2,1,0:T(8,128)}, bf16[3,384,1280]{2,1,0:T(8,128)(2,1)}) custom-call(f32[8,85,384]{2,1,0:T(8,128)} %reshape.7.spec, f32[4,2,136,136]{3,2,1,0:T(8,128)} %vc.1, s32[640]{0:T(1024)} %lat.1, f32[4,384]{1,0:T(4,128)} %band_filter.3, s32[4,12]{1,0:T(4,128)} %band_blocks.3, f32[20,384,640]{2,1,0:T(8,128)} %leg.1), custom_call_target="tpu_custom_call" | custom-call | tf_op jit(solution)/shard_map/pallas_call | solution.py:350
  47.7 0.0 copy-done
  47.7 0.6 convert_reduce_fusion.starts
  48.3 22.6 %shard_map.65.src = f32[8,85,384]{2,1,0:T(8,128)} custom-call(s32[40]{0:T(128)} %convert_reduce_fusion.starts, f32[4,384]{1,0:T(4,128)} %band_filter.3, s32[4,12]{1,0:T(4,128)} %band_blocks.3, f32[5,672,640]{2,1,0:T(8,128)} %get-tuple-element.8.g_hbm, bf16[3,384,1280]{2,1,0:T(8,128)(2,1)} %get-tuple-element.9.lp_hbm, f32[16,1248,128]{2,1,0:T(8,128)} %get-tuple-element.10.cov_hbm), custom_call_target="tpu_custom_call" | custom-call | tf_op jit(solution)/shard_map/pallas_call | solution.py:499
  71.0 17.0 %shard_map.66 = f32[40,17,384]{2,1,0:T(8,128)} custom-call(f32[8,85,384]{2,1,0:T(8,128)} %shard_map.65.src), custom_call_target="tpu_custom_call" | custom-call | tf_op jit(solution)/shard_map/pallas_call | solution.py:537
  88.0 2.9 %copy.14 = f32[20,2,17,384]{3,1,2,0:T(2,128)} copy(f32[20,2,17,384]{3,2,1,0:T(8,128)} %bitcast.5) | data formatting | bytes 2088960 | tf_op jit(solution)/shard_map/reshape | solution.py:552
Async XLA Ops:
  2.5 45.2 %copy-start = (s32[640]{0:T(1024)S(1)}, s32[640]{0:T(1024)}, u32[]{:S(2)}) copy-start(s32[640]{0:T(1024)} %lat.1) | copy-start | bytes 7684
